TPU v7x, 32 devices: a whole 2x2x4 slice. The times are simulated.
32 devices in a mesh: dp: 8 (over z, core), fsdp: 4 (over y, x).
Axes of the slice: x: 2, y: 2, z: 4, core: 2. Of those that a mesh axis runs over, the one named last changes fastest.
Arguments:
- tokens: bfloat16 [64, 384, 1024], P(('dp', 'fsdp')), may hold values from -6 to 6
- text_states: bfloat16 [64, 128, 1024], P(('dp', 'fsdp')), may hold values from -6 to 6
- caption_len: int32 [64], P(('dp', 'fsdp')), may hold values from 1 to 128, as said below
- out_grad: bfloat16 [64, 384, 1024], P(('dp', 'fsdp')), may hold values from -6 to 6
- norm1_gain: bfloat16 [1024], P(('dp', 'fsdp')), may hold values from 0.099609375 to 1.8984375
- norm1_bias: bfloat16 [1024], P(('dp', 'fsdp')), may hold values from -3 to 3
- qkv_weight: bfloat16 [1024, 3072], P(('dp', 'fsdp')), may hold values from -0.1875 to 0.1875
- self_out: bfloat16 [1024, 1024], P(('dp', 'fsdp')), may hold values from -0.75 to 0.75
- norm2_gain: bfloat16 [1024], P(('dp', 'fsdp')), may hold values from 0.099609375 to 1.8984375
- norm2_bias: bfloat16 [1024], P(('dp', 'fsdp')), may hold values from -3 to 3
- cross_query: bfloat16 [1024, 1024], P(('dp', 'fsdp')), may hold values from -0.1875 to 0.1875
- cross_kv: bfloat16 [1024, 2048], P(('dp', 'fsdp')), may hold values from -0.1875 to 0.1875
- cross_out: bfloat16 [1024, 1024], P(('dp', 'fsdp')), may hold values from -0.375 to 0.375
- norm3_gain: bfloat16 [1024], P(('dp', 'fsdp')), may hold values from 0.099609375 to 1.8984375
- norm3_bias: bfloat16 [1024], P(('dp', 'fsdp')), may hold values from -3 to 3
- ff_in: bfloat16 [1024, 4096], P(('dp', 'fsdp')), may hold values from -0.1875 to 0.1875
- ff_in_bias: bfloat16 [4096], P(('dp', 'fsdp')), may hold values from -3 to 3
- ff_out: bfloat16 [4096, 1024], P(('dp', 'fsdp')), may hold values from -0.09375 to 0.09375
- ff_out_bias: bfloat16 [1024], P(('dp', 'fsdp')), may hold values from -3 to 3
Outputs:
- result: bfloat16 [64, 384, 1024], P(('dp', 'fsdp'))
- tokens_grad: bfloat16 [64, 384, 1024], P(('dp', 'fsdp'))
- text_grad: bfloat16 [64, 128, 1024], P(('dp', 'fsdp'))
- norm1_gain_grad: float32 [1024], P(('dp', 'fsdp'))
- norm1_bias_grad: float32 [1024], P(('dp', 'fsdp'))
- qkv_weight_grad: float32 [1024, 3072], P(('dp', 'fsdp'))
- self_out_grad: float32 [1024, 1024], P(('dp', 'fsdp'))
- norm2_gain_grad: float32 [1024], P(('dp', 'fsdp'))
- norm2_bias_grad: float32 [1024], P(('dp', 'fsdp'))
- cross_query_grad: float32 [1024, 1024], P(('dp', 'fsdp'))
- cross_kv_grad: float32 [1024, 2048], P(('dp', 'fsdp'))
- cross_out_grad: float32 [1024, 1024], P(('dp', 'fsdp'))
- norm3_gain_grad: float32 [1024], P(('dp', 'fsdp'))
- norm3_bias_grad: float32 [1024], P(('dp', 'fsdp'))
- ff_in_grad: float32 [1024, 4096], P(('dp', 'fsdp'))
- ff_in_bias_grad: float32 [4096], P(('dp', 'fsdp'))
- ff_out_grad: float32 [4096, 1024], P(('dp', 'fsdp'))
- ff_out_bias_grad: float32 [1024], P(('dp', 'fsdp'))
Inputs may be any that keep to these rules, and one draw needn't show every extreme that they name: `caption_len`: each item's caption length; some item's is exactly 128.
All inputs are finite; a program needn't handle non-finite values.
Results may differ from a plain program's by a relative error of at most 0.017.
Values may be sent and summed in bfloat16 or wider, within the bound.
No kernel may reach another device: no remote copies, remote signals or barrier semaphores. Data moves between devices by JAX's collectives and lax.ppermute only.
A program may use at most 320 MiB of HBM per device.

v0:
```python
import jax
import jax.numpy as jnp
from jax import lax
from jax.sharding import PartitionSpec as P

HEADS = 16


EPSILON = 1e-05
NEGATIVE = -1e30


def fetch_weights(shards):
    return (
        lax.all_gather(shards[0], ("dp", "fsdp"), axis=0, tiled=True),
        lax.all_gather(shards[1], ("dp", "fsdp"), axis=0, tiled=True),
        lax.all_gather(shards[2], ("dp", "fsdp"), axis=0, tiled=True),
        lax.all_gather(shards[3], ("dp", "fsdp"), axis=0, tiled=True),
        lax.all_gather(shards[4], ("dp", "fsdp"), axis=0, tiled=True),
        lax.all_gather(shards[5], ("dp", "fsdp"), axis=0, tiled=True),
        lax.all_gather(shards[6], ("dp", "fsdp"), axis=0, tiled=True),
        lax.all_gather(shards[7], ("dp", "fsdp"), axis=0, tiled=True),
        lax.all_gather(shards[8], ("dp", "fsdp"), axis=0, tiled=True),
        lax.all_gather(shards[9], ("dp", "fsdp"), axis=0, tiled=True),
        lax.all_gather(shards[10], ("dp", "fsdp"), axis=0, tiled=True),
        lax.all_gather(shards[11], ("dp", "fsdp"), axis=0, tiled=True),
        lax.all_gather(shards[12], ("dp", "fsdp"), axis=0, tiled=True),
        lax.all_gather(shards[13], ("dp", "fsdp"), axis=0, tiled=True),
        lax.all_gather(shards[14], ("dp", "fsdp"), axis=0, tiled=True),
    )


def spread_grads(totals):
    return (
        lax.psum_scatter(totals[0], ("dp", "fsdp"), scatter_dimension=0, tiled=True),
        lax.psum_scatter(totals[1], ("dp", "fsdp"), scatter_dimension=0, tiled=True),
        lax.psum_scatter(totals[2], ("dp", "fsdp"), scatter_dimension=0, tiled=True),
        lax.psum_scatter(totals[3], ("dp", "fsdp"), scatter_dimension=0, tiled=True),
        lax.psum_scatter(totals[4], ("dp", "fsdp"), scatter_dimension=0, tiled=True),
        lax.psum_scatter(totals[5], ("dp", "fsdp"), scatter_dimension=0, tiled=True),
        lax.psum_scatter(totals[6], ("dp", "fsdp"), scatter_dimension=0, tiled=True),
        lax.psum_scatter(totals[7], ("dp", "fsdp"), scatter_dimension=0, tiled=True),
        lax.psum_scatter(totals[8], ("dp", "fsdp"), scatter_dimension=0, tiled=True),
        lax.psum_scatter(totals[9], ("dp", "fsdp"), scatter_dimension=0, tiled=True),
        lax.psum_scatter(totals[10], ("dp", "fsdp"), scatter_dimension=0, tiled=True),
        lax.psum_scatter(totals[11], ("dp", "fsdp"), scatter_dimension=0, tiled=True),
        lax.psum_scatter(totals[12], ("dp", "fsdp"), scatter_dimension=0, tiled=True),
        lax.psum_scatter(totals[13], ("dp", "fsdp"), scatter_dimension=0, tiled=True),
        lax.psum_scatter(totals[14], ("dp", "fsdp"), scatter_dimension=0, tiled=True),
    )


def norm_forward(values, gain, bias):
    center = values - jnp.mean(values, axis=-1, keepdims=True)
    inverse = lax.rsqrt(jnp.mean(center * center, axis=-1, keepdims=True) + EPSILON)
    scaled = center * inverse
    return (scaled * gain.astype(jnp.float32) + bias.astype(jnp.float32), scaled, inverse)


def norm_backward(upstream, scaled, inverse, gain):
    gain_grad = jnp.sum(upstream * scaled, axis=0)
    bias_grad = jnp.sum(upstream, axis=0)
    weighted = upstream * gain.astype(jnp.float32)
    input_grad = inverse * (
        weighted
        - jnp.mean(weighted, axis=-1, keepdims=True)
        - scaled * jnp.mean(weighted * scaled, axis=-1, keepdims=True)
    )
    return (input_grad, gain_grad, bias_grad)


def split_heads(matrix):
    return matrix.reshape(matrix.shape[0], HEADS, matrix.shape[1] // HEADS)


def product(first_matrix, second_matrix):
    return jnp.dot(first_matrix, second_matrix, preferred_element_type=jnp.float32)


def weight_grad(inputs, grads):
    return jnp.einsum("sa,sb->ab", inputs, grads, preferred_element_type=jnp.float32)


def input_grad_of(grads, weight):
    return jnp.einsum("sb,ab->sa", grads, weight, preferred_element_type=jnp.float32)


def attention_scores(query_rows, key_rows, allowed):
    scaling = (query_rows.shape[1] // HEADS) ** (-0.5)
    raw_scores = (
        jnp.einsum(
            "qhd,khd->hqk",
            split_heads(query_rows),
            split_heads(key_rows),
            preferred_element_type=jnp.float32,
        )
        * scaling
    )
    return jnp.where(allowed[None], raw_scores, NEGATIVE)


def attention_forward(query_rows, key_rows, value_rows, allowed):
    scores = attention_scores(query_rows, key_rows, allowed)
    row_max = jnp.max(scores, axis=-1, keepdims=True)
    weights = jnp.exp(scores - row_max)
    exp_total = jnp.sum(weights, axis=-1, keepdims=True)
    probability = (weights / exp_total).astype(jnp.bfloat16)
    attended = jnp.einsum(
        "hqk,khd->qhd", probability, split_heads(value_rows), preferred_element_type=jnp.float32
    )
    return (
        attended.reshape(query_rows.shape[0], -1).astype(jnp.bfloat16),
        row_max + jnp.log(exp_total),
    )


def attention_backward(attended_grad, query_rows, key_rows, value_rows, allowed, log_total):
    scaling = (query_rows.shape[1] // HEADS) ** (-0.5)
    probability = jnp.exp(attention_scores(query_rows, key_rows, allowed) - log_total)
    rounded = probability.astype(jnp.bfloat16)
    grad_heads = split_heads(attended_grad)
    value_grad = jnp.einsum("hqk,qhd->khd", rounded, grad_heads, preferred_element_type=jnp.float32)
    prob_grad = jnp.einsum(
        "qhd,khd->hqk", grad_heads, split_heads(value_rows), preferred_element_type=jnp.float32
    )
    score_grad = (
        probability * (prob_grad - jnp.sum(prob_grad * probability, axis=-1, keepdims=True))
    ).astype(jnp.bfloat16)
    query_grad = (
        jnp.einsum(
            "hqk,khd->qhd", score_grad, split_heads(key_rows), preferred_element_type=jnp.float32
        )
        * scaling
    )
    key_grad = (
        jnp.einsum(
            "hqk,qhd->khd", score_grad, split_heads(query_rows), preferred_element_type=jnp.float32
        )
        * scaling
    )
    return (
        query_grad.reshape(query_rows.shape[0], -1),
        key_grad.reshape(key_rows.shape[0], -1),
        value_grad.reshape(key_rows.shape[0], -1),
    )


def forward(gathered, token_rows, text_rows, caption_length):
    (
        norm1_gain,
        norm1_bias,
        qkv_weight,
        self_out,
        norm2_gain,
        norm2_bias,
        cross_query,
        cross_kv,
        cross_out,
        norm3_gain,
        norm3_bias,
        ff_in,
        ff_in_bias,
        ff_out,
        ff_out_bias,
    ) = gathered
    row_count = token_rows.shape[0]
    model_width = token_rows.shape[1]
    token_values = token_rows.astype(jnp.float32)
    normed_one, scaled_one, inverse_one = norm_forward(token_values, norm1_gain, norm1_bias)
    normed_one = normed_one.astype(jnp.bfloat16)
    projected = product(normed_one, qkv_weight).astype(jnp.bfloat16)
    causal = lax.broadcasted_iota(jnp.int32, (row_count, row_count), 0) >= lax.broadcasted_iota(
        jnp.int32, (row_count, row_count), 1
    )
    attended_one, total_one = attention_forward(
        projected[:, :model_width],
        projected[:, model_width : 2 * model_width],
        projected[:, 2 * model_width :],
        causal,
    )
    after_self = token_values + product(attended_one, self_out)
    normed_two, scaled_two, inverse_two = norm_forward(after_self, norm2_gain, norm2_bias)
    normed_two = normed_two.astype(jnp.bfloat16)
    query_two = product(normed_two, cross_query).astype(jnp.bfloat16)
    text_kv = product(text_rows, cross_kv).astype(jnp.bfloat16)
    visible = lax.broadcasted_iota(jnp.int32, (row_count, text_rows.shape[0]), 1) < caption_length
    attended_two, total_two = attention_forward(
        query_two, text_kv[:, :model_width], text_kv[:, model_width:], visible
    )
    after_cross = after_self + product(attended_two, cross_out)
    normed_three, scaled_three, inverse_three = norm_forward(after_cross, norm3_gain, norm3_bias)
    normed_three = normed_three.astype(jnp.bfloat16)
    before = product(normed_three, ff_in) + ff_in_bias.astype(jnp.float32)
    middle = jax.nn.gelu(before, approximate=True).astype(jnp.bfloat16)
    outcome = (after_cross + (product(middle, ff_out) + ff_out_bias.astype(jnp.float32))).astype(
        jnp.bfloat16
    )
    kept_state = (
        normed_one,
        scaled_one,
        inverse_one,
        projected,
        causal,
        attended_one,
        total_one,
        normed_two,
        scaled_two,
        inverse_two,
        query_two,
        text_kv,
        visible,
        attended_two,
        total_two,
        normed_three,
        scaled_three,
        inverse_three,
        before,
        middle,
    )
    return (outcome, kept_state)


def backward(gathered, kept_state, text_rows, cotangent):
    (
        norm1_gain,
        norm1_bias,
        qkv_weight,
        self_out,
        norm2_gain,
        norm2_bias,
        cross_query,
        cross_kv,
        cross_out,
        norm3_gain,
        norm3_bias,
        ff_in,
        ff_in_bias,
        ff_out,
        ff_out_bias,
    ) = gathered
    (
        normed_one,
        scaled_one,
        inverse_one,
        projected,
        causal,
        attended_one,
        total_one,
        normed_two,
        scaled_two,
        inverse_two,
        query_two,
        text_kv,
        visible,
        attended_two,
        total_two,
        normed_three,
        scaled_three,
        inverse_three,
        before,
        middle,
    ) = kept_state
    model_width = normed_one.shape[1]
    ff_out_bias_grad = jnp.sum(cotangent.astype(jnp.float32), axis=0)
    ff_out_grad = weight_grad(middle, cotangent)
    middle_grad = input_grad_of(cotangent, ff_out)
    gelu_pull = jax.vjp(lambda values: jax.nn.gelu(values, approximate=True), before)[1]
    before_grad = gelu_pull(middle_grad)[0].astype(jnp.bfloat16)
    ff_in_bias_grad = jnp.sum(before_grad.astype(jnp.float32), axis=0)
    ff_in_grad = weight_grad(normed_three, before_grad)
    norm_input, norm3_gain_grad, norm3_bias_grad = norm_backward(
        input_grad_of(before_grad, ff_in), scaled_three, inverse_three, norm3_gain
    )
    cross_grad = cotangent.astype(jnp.float32) + norm_input
    cross_round = cross_grad.astype(jnp.bfloat16)
    cross_out_grad = weight_grad(attended_two, cross_round)
    attended_two_grad = input_grad_of(cross_round, cross_out).astype(jnp.bfloat16)
    query_grad, key_grad, value_grad = attention_backward(
        attended_two_grad,
        query_two,
        text_kv[:, :model_width],
        text_kv[:, model_width:],
        visible,
        total_two,
    )
    query_two_grad = query_grad.astype(jnp.bfloat16)
    text_kv_grad = jnp.concatenate([key_grad, value_grad], axis=1).astype(jnp.bfloat16)
    cross_query_grad = weight_grad(normed_two, query_two_grad)
    cross_kv_grad = weight_grad(text_rows, text_kv_grad)
    text_grad = input_grad_of(text_kv_grad, cross_kv).astype(jnp.bfloat16)
    norm_input, norm2_gain_grad, norm2_bias_grad = norm_backward(
        input_grad_of(query_two_grad, cross_query), scaled_two, inverse_two, norm2_gain
    )
    self_grad = cross_grad + norm_input
    self_round = self_grad.astype(jnp.bfloat16)
    self_out_grad = weight_grad(attended_one, self_round)
    attended_one_grad = input_grad_of(self_round, self_out).astype(jnp.bfloat16)
    query_grad, key_grad, value_grad = attention_backward(
        attended_one_grad,
        projected[:, :model_width],
        projected[:, model_width : 2 * model_width],
        projected[:, 2 * model_width :],
        causal,
        total_one,
    )
    projected_grad = jnp.concatenate([query_grad, key_grad, value_grad], axis=1).astype(
        jnp.bfloat16
    )
    qkv_weight_grad = weight_grad(normed_one, projected_grad)
    norm_input, norm1_gain_grad, norm1_bias_grad = norm_backward(
        input_grad_of(projected_grad, qkv_weight), scaled_one, inverse_one, norm1_gain
    )
    tokens_grad = (self_grad + norm_input).astype(jnp.bfloat16)
    grad_terms = (
        norm1_gain_grad,
        norm1_bias_grad,
        qkv_weight_grad,
        self_out_grad,
        norm2_gain_grad,
        norm2_bias_grad,
        cross_query_grad,
        cross_kv_grad,
        cross_out_grad,
        norm3_gain_grad,
        norm3_bias_grad,
        ff_in_grad,
        ff_in_bias_grad,
        ff_out_grad,
        ff_out_bias_grad,
    )
    return (grad_terms, tokens_grad, text_grad)


def per_device(
    tokens,
    text_states,
    caption_len,
    out_grad,
    norm1_gain,
    norm1_bias,
    qkv_weight,
    self_out,
    norm2_gain,
    norm2_bias,
    cross_query,
    cross_kv,
    cross_out,
    norm3_gain,
    norm3_bias,
    ff_in,
    ff_in_bias,
    ff_out,
    ff_out_bias,
):
    shards = (
        norm1_gain,
        norm1_bias,
        qkv_weight,
        self_out,
        norm2_gain,
        norm2_bias,
        cross_query,
        cross_kv,
        cross_out,
        norm3_gain,
        norm3_bias,
        ff_in,
        ff_in_bias,
        ff_out,
        ff_out_bias,
    )
    totals = None
    outcomes = []
    token_grads = []
    text_grads = []
    for batch_index in range(tokens.shape[0]):
        current = fetch_weights(shards)
        outcome, kept_state = forward(
            current, tokens[batch_index], text_states[batch_index], caption_len[batch_index]
        )
        current = fetch_weights(shards)
        grad_terms, token_grad, text_grad = backward(
            current, kept_state, text_states[batch_index], out_grad[batch_index]
        )
        if totals is None:
            totals = grad_terms
        else:
            totals = tuple((earlier + latest for earlier, latest in zip(totals, grad_terms)))
        outcomes.append(outcome)
        token_grads.append(token_grad)
        text_grads.append(text_grad)
    owned_rows = spread_grads(totals)
    return (
        jnp.stack(outcomes),
        jnp.stack(token_grads),
        jnp.stack(text_grads),
        owned_rows[0],
        owned_rows[1],
        owned_rows[2],
        owned_rows[3],
        owned_rows[4],
        owned_rows[5],
        owned_rows[6],
        owned_rows[7],
        owned_rows[8],
        owned_rows[9],
        owned_rows[10],
        owned_rows[11],
        owned_rows[12],
        owned_rows[13],
        owned_rows[14],
    )


def solution(mesh):
    placed = (
        P(("dp", "fsdp"), None, None),
        P(("dp", "fsdp"), None, None),
        P(("dp", "fsdp")),
        P(("dp", "fsdp"), None, None),
        P(("dp", "fsdp")),
        P(("dp", "fsdp")),
        P(("dp", "fsdp"), None),
        P(("dp", "fsdp"), None),
        P(("dp", "fsdp")),
        P(("dp", "fsdp")),
        P(("dp", "fsdp"), None),
        P(("dp", "fsdp"), None),
        P(("dp", "fsdp"), None),
        P(("dp", "fsdp")),
        P(("dp", "fsdp")),
        P(("dp", "fsdp"), None),
        P(("dp", "fsdp")),
        P(("dp", "fsdp"), None),
        P(("dp", "fsdp")),
    )
    return jax.shard_map(
        per_device,
        mesh=mesh,
        in_specs=placed,
        out_specs=(
            P(("dp", "fsdp"), None, None),
            P(("dp", "fsdp"), None, None),
            P(("dp", "fsdp"), None, None),
            P(("dp", "fsdp")),
            P(("dp", "fsdp")),
            P(("dp", "fsdp"), None),
            P(("dp", "fsdp"), None),
            P(("dp", "fsdp")),
            P(("dp", "fsdp")),
            P(("dp", "fsdp"), None),
            P(("dp", "fsdp"), None),
            P(("dp", "fsdp"), None),
            P(("dp", "fsdp")),
            P(("dp", "fsdp")),
            P(("dp", "fsdp"), None),
            P(("dp", "fsdp")),
            P(("dp", "fsdp"), None),
            P(("dp", "fsdp")),
        ),
        check_vma=False,
    )
```

profile of v0, /device:TPU:0, one launch (start us, length us, event | category | flops | bytes accessed | tf_op | source)
XLA Modules:
  0.0 2091.9 jit_solution(4631893387749233506)
XLA Ops:
  17.8 42.2 %all-reduce.16 = (bf16[1024]{0:T(1024)(128)(2,1)S(1)}, bf16[1024]{0:T(1024)(128)(2,1)S(1)}, bf16[1024]{0:T(1024)(128)(2,1)S(1)}, bf16[1024]{0:T(1024)(128)(2,1)S...) all-reduce(bf16[1024]{0:T(1024)(128)(2,1)S(1)} %dynamic-update-slic, ...), channel_id=1, replica_groups=mesh['dp'=8,'fsdp'=4] {'dp','fsdp'}, use_global_device_ids=true, to_apply=%add.1 | all-reduce | flops 7168 | bytes 28672
  63.0 66.3 %all-gather = bf16[32,1,128]{2,1,0:T(2,128)(2,1)S(1)} all-gather(bf16[1,1,128]{2,1,0:T(2,128)(2,1)} %bitcast.349), channel_id=1, replica_groups=mesh['dp'=8,'fsdp'=4] {'dp','fsdp'}, dimensions={0}, use_global_device_ids=true | all-gather | bytes 8448 | tf_op jit(solution)/shard_map/all_gather | solution.py:27
  146.6 6.0 convolution_convert_fusion
  155.2 5.9 convolution_convert_fusion.1
  173.5 7.3 fusion
  181.4 4.1 fusion.77
  185.5 19.3 all-gather.11.cloned.1.call-done
  208.0 54.7 %all-gather.15.cloned.1.call-done = bf16[1024,1024]{1,0:T(8,128)(2,1)} async-done(((bf16[32,1024]{1,0:T(8,128)(2,1)}), bf16[1024,1024]{1,0:T(8,128)(2,1)}) %all-gather.15.cloned.1.call-update) | async-done | bytes 2097168 | tf_op jit(solution)/shard_map/all_gather | solution.py:21
  271.8 49.0 %all-gather.17.cloned.1.call-done = bf16[1024,1024]{1,0:T(8,128)(2,1)} async-done(((bf16[32,1024]{1,0:T(8,128)(2,1)}), bf16[1024,1024]{1,0:T(8,128)(2,1)}) %all-gather.17.cloned.1.call-update) | async-done | bytes 2097168 | tf_op jit(solution)/shard_map/all_gather | solution.py:23
  320.8 3.4 fusion.164
  327.5 72.5 %all-gather.19.cloned.1.call-done = bf16[1024,4096]{1,0:T(8,128)(2,1)} async-done(((bf16[32,4096]{1,0:T(8,128)(2,1)}), bf16[1024,4096]{1,0:T(8,128)(2,1)}) %all-gather.19.cloned.1.call-update) | async-done | bytes 8388624 | tf_op jit(solution)/shard_map/all_gather | solution.py:26
  399.9 10.0 convolution_add_fusion.4
  410.0 69.0 %all-gather.21.cloned.1.call-done = bf16[4096,1024]{1,0:T(8,128)(2,1)} async-done(((bf16[128,1024]{1,0:T(8,128)(2,1)}), bf16[4096,1024]{1,0:T(8,128)(2,1)}) %all-gather.21.cloned.1.call-update) | async-done | bytes 8388624 | tf_op jit(solution)/shard_map/all_gather | solution.py:28
  479.0 11.6 convert_reduce_fusion.1
  490.6 4.5 multiply_reduce_fusion.5
  517.2 16.1 multiply_reduce_fusion.1
  548.2 3.6 convolution_add_fusion.3
  551.8 12.2 convert_reduce_fusion
  564.0 8.1 multiply_reduce_fusion.4
  589.2 3.3 convolution_add_fusion.7
  593.2 3.2 fusion.155
  596.4 3.5 convolution_add_fusion.6
  603.3 3.4 convolution_add_fusion.5
  606.8 4.0 convolution_convert_fusion.4
  613.1 10.7 multiply_reduce_fusion
  623.8 14.6 multiply_convert_fusion.1
  644.9 6.6 fusion.78
  651.5 3.8 fusion.97
  655.4 3.5 fusion.81
  658.9 10.1 convolution_add_fusion.2
  678.3 4.6 add_bitcast_fusion
  682.9 9.2 copy.168
  693.5 10.4 fusion.156
  703.9 11.8 convolution_add_fusion.1
  717.2 11.9 fusion.106
  729.1 18.5 convolution_add_fusion
  748.3 6.3 fusion.96
  754.8 8.3 fusion.64
  763.2 41.0 %all-reduce.15 = (f32[1024]{0:T(1024)S(1)}, f32[1024]{0:T(1024)S(1)}, f32[1024]{0:T(1024)S(1)}, f32[1024]{0:T(1024)S(1)}, f32[1024]{0:T(1024)S(1)}, /*index=5*/f...) all-reduce(f32[1024]{0:T(1024)S(1)} %add.323, ...), channel_id=2, replica_groups=mesh['dp'=8,'fsdp'=4] {'dp','fsdp'}, use_global_device_ids=true, to_apply=%region_38.39.clone | all-reduce | flops 11264 | bytes 90112
  808.9 4.0 fusion.95
  815.4 9.5 fusion.85
  825.0 4.0 fusion.84
  834.1 40.5 %reduce-scatter.14.cloned.1.call-done = f32[32,1024]{1,0:T(8,128)} async-done(((f32[1024,1024]{1,0:T(8,128)}), f32[32,1024]{1,0:T(8,128)}) %reduce-scatter.14.cloned.1.call-update) | async-done | bytes 131088 | tf_op jit(solution)/shard_map/reduce_scatter | solution.py:41
  874.6 141.9 %reduce-scatter.16.cloned.1.call-done = f32[32,1024]{1,0:T(8,128)} async-done(((f32[1024,1024]{1,0:T(8,128)}), f32[32,1024]{1,0:T(8,128)}) %reduce-scatter.16.cloned.1.call-update) | async-done | bytes 131088 | tf_op jit(solution)/shard_map/reduce_scatter | solution.py:43
  1016.5 159.7 %reduce-scatter.10.cloned.1.call-done = f32[32,3072]{1,0:T(8,128)} async-done(((f32[1024,3072]{1,0:T(8,128)}), f32[32,3072]{1,0:T(8,128)}) %reduce-scatter.10.cloned.1.call-update) | async-done | bytes 393232 | tf_op jit(solution)/shard_map/reduce_scatter | solution.py:37
  1176.2 185.4 %reduce-scatter.22.cloned.1.call-done = f32[32,2048]{1,0:T(8,128)} async-done(((f32[1024,2048]{1,0:T(8,128)}), f32[32,2048]{1,0:T(8,128)}) %reduce-scatter.22.cloned.1.call-update) | async-done | bytes 262160
  1361.6 361.6 %reduce-scatter.18.cloned.1.call-done = f32[32,4096]{1,0:T(8,128)} async-done(((f32[1024,4096]{1,0:T(8,128)}), f32[32,4096]{1,0:T(8,128)}) %reduce-scatter.18.cloned.1.call-update) | async-done | bytes 524304 | tf_op jit(solution)/shard_map/reduce_scatter | solution.py:46
  1723.2 361.9 %reduce-scatter.20.cloned.1.call-done = f32[128,1024]{1,0:T(8,128)} async-done(((f32[4096,1024]{1,0:T(8,128)}), f32[128,1024]{1,0:T(8,128)}) %reduce-scatter.20.cloned.1.call-update) | async-done | bytes 524304 | tf_op jit(solution)/shard_map/reduce_scatter | solution.py:48
  (535 shorter events, 152.6 us)
Async XLA Ops:
  7.2 128.7 %copy-start.5 = (bf16[2,384,1024]{2,1,0:T(8,128)(2,1)S(1)}, bf16[2,384,1024]{2,1,0:T(8,128)(2,1)}, u32[]{:S(2)}) copy-start(bf16[2,384,1024]{2,1,0:T(8,128)(2,1)} %param.19) | copy-start | bytes 4718596
  7.2 130.5 %copy-start.74 = (bf16[2,128,1024]{2,1,0:T(8,128)(2,1)S(1)}, bf16[2,128,1024]{2,1,0:T(8,128)(2,1)}, u32[]{:S(2)}) copy-start(bf16[2,128,1024]{2,1,0:T(8,128)(2,1)} %param.20) | copy-start | bytes 1572868
  7.2 130.4 %all-gather.13.cloned.1.call-start = ((), (), s32[]{:S(2)}) async-start(), calls=%async_computation.9 | async-start | bytes 4325376 | tf_op jit(solution)/shard_map/all_gather | solution.py:22
  7.9 138.6 %all-gather.9.cloned.1.call-start = ((), (), s32[]{:S(2)}) async-start(), calls=%async_computation.7 | async-start | bytes 6488064 | tf_op jit(solution)/shard_map/all_gather | solution.py:17
  8.7 196.1 %all-gather.11.cloned.1.call-start = ((), (), s32[]{:S(2)}) async-start(), calls=%async_computation.8 | async-start | bytes 2162688 | tf_op jit(solution)/shard_map/all_gather | solution.py:18
  9.4 253.3 %all-gather.15.cloned.1.call-start = ((), (), s32[]{:S(2)}) async-start(), calls=%async_computation.10 | async-start | bytes 2162688 | tf_op jit(solution)/shard_map/all_gather | solution.py:21
  10.0 310.8 %all-gather.17.cloned.1.call-start = ((), (), s32[]{:S(2)}) async-start(), calls=%async_computation.11 | async-start | bytes 2162688 | tf_op jit(solution)/shard_map/all_gather | solution.py:23
  10.6 389.3 %all-gather.19.cloned.1.call-start = ((), (), s32[]{:S(2)}) async-start(), calls=%async_computation.12 | async-start | bytes 8650752 | tf_op jit(solution)/shard_map/all_gather | solution.py:26
  11.2 467.8 %all-gather.21.cloned.1.call-start = ((), (), s32[]{:S(2)}) async-start(), calls=%async_computation.13 | async-start | bytes 8650752 | tf_op jit(solution)/shard_map/all_gather | solution.py:28
  11.9 822.1 %reduce-scatter.12.cloned.1.call-start = ((), (), s32[]{:S(2)}) async-start(), calls=%async_computation.15 | async-start | bytes 4325376 | tf_op jit(solution)/shard_map/reduce_scatter | solution.py:38
  207.7 57.7 %copy-start.3 = (f32[384,1024]{1,0:T(8,128)}, f32[384,1024]{1,0:T(8,128)S(1)}, u32[]{:S(2)}) copy-start(f32[384,1024]{1,0:T(8,128)S(1)} %get-tuple-element.144) | copy-start | bytes 4718596
  207.7 57.7 %copy-start.123 = (f32[384]{0:T(512)}, f32[384]{0:T(512)S(1)}, u32[]{:S(2)}) copy-start(f32[384]{0:T(512)S(1)} %broadcast_multiply_fusion.16) | copy-start | bytes 4612
  208.0 57.4 %copy-start.133 = (f32[384]{0:T(512)}, f32[384]{0:T(512)S(1)}, u32[]{:S(2)}) copy-start(f32[384]{0:T(512)S(1)} %add_rsqrt_fusion.4) | copy-start | bytes 4612
  268.7 234.4 %copy-start = (f32[16,384,128]{1,2,0:T(8,128)}, f32[16,384,128]{1,2,0:T(8,128)S(1)}, u32[]{:S(2)}) copy-start(f32[16,384,128]{1,2,0:T(8,128)S(1)} %get-tuple-element.146) | copy-start | bytes 9437188
  479.0 11.6 copy-start.18
  479.0 11.6 copy-start.81
  479.0 11.6 copy-start.107
  479.0 11.6 copy-start.119
  479.0 11.6 copy-start.163
  512.9 20.4 slice-start
  517.2 16.1 slice-start.1
  517.2 16.1 slice-start.2
  517.2 16.1 copy-start.51
  517.2 16.1 copy-start.140
  547.8 24.3 %copy-start.15 = (f32[384,1024]{1,0:T(8,128)}, f32[384,1024]{1,0:T(8,128)S(1)}, u32[]{:S(2)}) copy-start(f32[384,1024]{1,0:T(8,128)S(1)} %get-tuple-element.159) | copy-start | bytes 4718596
  547.8 24.3 %copy-start.121 = (f32[384]{0:T(512)}, f32[384]{0:T(512)S(1)}, u32[]{:S(2)}) copy-start(f32[384]{0:T(512)S(1)} %broadcast_multiply_fusion.12) | copy-start | bytes 4612
  548.2 23.9 %copy-start.131 = (f32[384]{0:T(512)}, f32[384]{0:T(512)S(1)}, u32[]{:S(2)}) copy-start(f32[384]{0:T(512)S(1)} %add_rsqrt_fusion) | copy-start | bytes 4612
  551.8 12.2 copy-start.21
  592.5 282.1 %reduce-scatter.14.cloned.1.call-start = ((), (), s32[]{:S(2)}) async-start(), calls=%async_computation.16 | async-start | bytes 4325376 | tf_op jit(solution)/shard_map/reduce_scatter | solution.py:41
  600.0 416.5 %reduce-scatter.16.cloned.1.call-start = ((), (), s32[]{:S(2)}) async-start(), calls=%async_computation.17 | async-start | bytes 4325376 | tf_op jit(solution)/shard_map/reduce_scatter | solution.py:43
  606.7 569.5 %reduce-scatter.10.cloned.1.call-start = ((), (), s32[]{:S(2)}) async-start(), calls=%async_computation.14 | async-start | bytes 12976128 | tf_op jit(solution)/shard_map/reduce_scatter | solution.py:37
  613.1 10.7 copy-start.112
  613.1 10.7 copy-start.139
  623.8 14.6 copy-start.57
  640.2 18.7 copy-start.63
  641.1 17.8 copy-start.64
  644.9 10.5 slice-start.3
  644.9 10.5 slice-start.4
  669.0 692.6 %reduce-scatter.22.cloned.1.call-start = ((), (), s32[]{:S(2)}) async-start(), calls=%async_computation.20 | async-start | bytes 8650752
  692.1 11.8 copy-start.16
  692.1 11.8 copy-start.122
  692.2 11.8 copy-start.132
  692.2 1031.1 %reduce-scatter.18.cloned.1.call-start = ((), (), s32[]{:S(2)}) async-start(), calls=%async_computation.18 | async-start | bytes 17301504 | tf_op jit(solution)/shard_map/reduce_scatter | solution.py:46
  693.5 10.4 copy-start.55
  715.8 1369.3 %reduce-scatter.20.cloned.1.call-start = ((), (), s32[]{:S(2)}) async-start(), calls=%async_computation.19 | async-start | bytes 17301504 | tf_op jit(solution)/shard_map/reduce_scatter | solution.py:48
  813.0 11.9 slice-start.6
  813.0 11.9 slice-start.10
  815.4 9.6 slice-start.11
  (145 other events, 550.7 us)
Sparse Core Ops, SparseCore 0:
  10.9 64.9 all-gather.12
  78.8 67.6 all-gather.8
  149.3 55.3 all-gather.10
  207.5 55.2 all-gather.14
  265.5 55.2 all-gather.16
  323.5 76.3 all-gather.18
  402.8 76.1 all-gather.20
  592.6 140.2 reduce-scatter.11
  735.8 138.7 reduce-scatter.13
  877.3 139.1 reduce-scatter.15
  1023.1 153.0 reduce-scatter.9
  1179.0 182.5 reduce-scatter.21
  1364.6 358.5 reduce-scatter.17
  1726.1 359.0 reduce-scatter.19
where the time goes:
time: 2100 us; the launch traced here: 2090 us
  waiting for transfers between devices  1520 us (72%)
  matrix products  295 us (14%)
  blocking collectives  150 us (7%)
  local copies, waits for them, and re-layouts  71.4 us (3%)
  other arithmetic  38.6 us (2%)
    reduce_scatter x1, waiting for transfers between devices, spread_grads(): lax.psum_scatter(totals[13], ('dp', 'fsdp'), scatter_dimension=0, tiled=T...  362 us
    reduce_scatter x1, waiting for transfers between devices, spread_grads(): lax.psum_scatter(totals[11], ('dp', 'fsdp'), scatter_dimension=0, tiled=T...  362 us
    unnamed x15, waiting for transfers between devices  190 us
    reduce_scatter x1, waiting for transfers between devices, spread_grads(): lax.psum_scatter(totals[2], ('dp', 'fsdp'), scatter_dimension=0, tiled=True)  160 us
    reduce_scatter x1, waiting for transfers between devices, spread_grads(): lax.psum_scatter(totals[8], ('dp', 'fsdp'), scatter_dimension=0, tiled=True)  142 us
    dot_general x14, matrix products, weight_grad(): jnp.einsum('sa,sb->ab', inputs, grads, preferred_element_type=jnp.float32)  91.9 us
    unnamed x2, blocking collectives  83.2 us
    all_gather x1, waiting for transfers between devices, fetch_weights(): lax.all_gather(shards[11], ('dp', 'fsdp'), axis=0, tiled=True)  72.5 us
  transfers between devices with their start and end apart: 14, of which 11 were waited for; matrix products, arithmetic and copies ran while one was open for 13% of the time, Pallas kernels for 0%

commit v1 on v0

v1 whole, which is shorter than its diff:
```python
import functools

import jax
import jax.numpy as jnp
from jax import lax
from jax.experimental import pallas as pl
from jax.experimental.pallas import tpu as pltpu
from jax.sharding import PartitionSpec as P

HEADS = 16
EPSILON = 1e-05
NEGATIVE = -1e30
AXES = ("dp", "fsdp")
F32 = jnp.float32
BF16 = jnp.bfloat16


class Place:
    def __init__(self, line_count, plane_count):
        self.lines = line_count
        self.planes = plane_count
        self.bits = [1 << k for k in range(plane_count.bit_length() - 1)]
        dp = lax.axis_index("dp")
        self.line = dp // 2
        self.core = dp % 2
        self.plane = lax.axis_index("fsdp")

    def _pairs(self, target):
        pairs = []
        for line in range(self.lines):
            for core in range(2):
                for plane in range(self.planes):
                    l, c, p = target(line, core, plane)
                    pairs.append(
                        (
                            (line * 2 + core) * self.planes + plane,
                            (l * 2 + c) * self.planes + p,
                        )
                    )
        return pairs

    def shift_line(self, value, step):
        return lax.ppermute(
            value, AXES, self._pairs(lambda l, c, p: ((l + step) % self.lines, c, p))
        )

    def swap_plane(self, value, bit):
        return lax.ppermute(value, AXES, self._pairs(lambda l, c, p: (l, c, p ^ bit)))

    def swap_core(self, value):
        return lax.ppermute(value, AXES, self._pairs(lambda l, c, p: (l, 1 - c, p)))


def interleave(pieces, slots):
    count = len(pieces)
    outer, rows, width = pieces[0].shape
    tile = 2048 if width % 2048 == 0 else 1024

    def body(slots_ref, *refs):
        out_ref = refs[count]
        for k in range(count):
            out_ref[0, pl.ds(slots_ref[k], 1)] = refs[k][...]

    return pl.pallas_call(
        body,
        out_shape=jax.ShapeDtypeStruct((outer, count, rows, width), pieces[0].dtype),
        grid_spec=pltpu.PrefetchScalarGridSpec(
            num_scalar_prefetch=1,
            grid=(outer, width // tile),
            in_specs=[pl.BlockSpec((1, rows, tile), lambda a, n, s: (a, 0, n))] * count,
            out_specs=pl.BlockSpec((1, count, rows, tile), lambda a, n, s: (a, 0, 0, n)),
        ),
        name="interleave",
    )(slots.astype(jnp.int32), *pieces)


def gather(place, shard, order):
    rows, width = shard.shape
    steps = [shard] + [place.shift_line(shard, s) for s in range(1, place.lines)]
    held = interleave(
        [piece[None] for piece in steps],
        (place.line - jnp.arange(place.lines)) % place.lines,
    ).reshape(place.lines, rows, width)
    pieces, masks = [held], [0]
    for bit in order:
        pieces = pieces + [place.swap_plane(piece, bit) for piece in pieces]
        masks = masks + [mask ^ bit for mask in masks]
    half = interleave(pieces, jnp.array(masks) ^ place.plane)
    half = half.reshape(place.lines, place.planes * rows, width)
    other = place.swap_core(half)
    return interleave([half, other], jnp.array([0, 1]) ^ place.core)


def gather_small(place, shard):
    line_pieces = jnp.stack(
        [shard] + [place.shift_line(shard, s) for s in range(1, place.lines)]
    )
    held = line_pieces[(place.line - jnp.arange(place.lines)) % place.lines]
    pieces, masks = held[None], [0]
    for bit in place.bits:
        pieces = jnp.concatenate([pieces, place.swap_plane(pieces, bit)])
        masks = masks + [mask ^ bit for mask in masks]
    inverse = [masks.index(m) for m in range(len(masks))]
    half = pieces[jnp.array(inverse)[jnp.arange(place.planes) ^ place.plane]]
    both = jnp.stack([half, place.swap_core(half)])[jnp.arange(2) ^ place.core]
    return both.transpose(2, 0, 1, 3, 4)[:, :, :, 0]


def scatter(place, terms, order, kind):
    width = terms.shape[1]
    rows = terms.shape[0] // (place.lines * 2 * place.planes)
    halves = terms.reshape(place.lines, 2, place.planes * rows, width)
    mine = lax.dynamic_index_in_dim(halves, place.core, 1, keepdims=False)
    other = lax.dynamic_index_in_dim(halves, 1 - place.core, 1, keepdims=False)
    arrived = place.swap_core(other.astype(kind))
    total = (mine.astype(F32) + arrived.astype(F32)).astype(kind)
    total = total.reshape(place.lines, place.planes, rows, width)
    parts = {
        mask: lax.dynamic_index_in_dim(total, place.plane ^ mask, 1, keepdims=False)
        for mask in range(place.planes)
    }
    for bit in reversed(order):
        kept = [mask for mask in parts if not mask & bit]
        arrivals = {mask: place.swap_plane(parts[mask ^ bit], bit) for mask in kept}
        parts = {
            mask: (parts[mask].astype(F32) + arrivals[mask].astype(F32)).astype(kind)
            for mask in kept
        }
    total = parts[0]
    result = lax.dynamic_index_in_dim(total, place.line, 0, keepdims=False).astype(F32)
    for step in range(1, place.lines):
        sent = lax.dynamic_index_in_dim(
            total, (place.line + step) % place.lines, 0, keepdims=False
        )
        result = result + place.shift_line(sent, step).astype(F32)
    return result


def nt(first, second):
    return lax.dot_general(first, second, (((1,), (1,)), ((), ())), preferred_element_type=F32)


def tn(first, second):
    return lax.dot_general(first, second, (((0,), (0,)), ((), ())), preferred_element_type=F32)


def nn(first, second):
    return lax.dot_general(first, second, (((1,), (0,)), ((), ())), preferred_element_type=F32)


def lanes_of(head, shape):
    lane = lax.broadcasted_iota(jnp.int32, shape, 1)
    return (lane >= head * (shape[1] // 2)) & (lane < (head + 1) * (shape[1] // 2))


def self_forward_body(query_ref, key_ref, value_ref, out_ref, lse_ref, *, scaling, block):
    rows, lanes = query_ref.shape[1:]
    for start in range(0, rows, block):
        seen = start + block
        total = None
        for head in range(2):
            query = query_ref[0, start:seen]
            query = jnp.where(lanes_of(head, query.shape), query * scaling, 0).astype(BF16)
            scores = nt(query, key_ref[0, :seen])
            row = lax.broadcasted_iota(jnp.int32, scores.shape, 0) + start
            column = lax.broadcasted_iota(jnp.int32, scores.shape, 1)
            scores = jnp.where(column <= row, scores, NEGATIVE)
            top = jnp.max(scores, axis=1, keepdims=True)
            weights = jnp.exp(scores - top)
            summed = jnp.sum(weights, axis=1, keepdims=True)
            probability = (weights * (1.0 / summed)).astype(BF16)
            value = value_ref[0, :seen]
            value = jnp.where(lanes_of(head, value.shape), value, 0).astype(BF16)
            part = nn(probability, value)
            total = part if total is None else total + part
            lse_ref[0, head, start:seen] = top + jnp.log(summed)
        out_ref[0, start:seen] = total.astype(BF16)


def self_attention(projected, heads):
    items, rows, triple = projected.shape
    pairs = heads // 2
    lanes = triple // 3 // pairs
    scaling = (triple // 3 // heads) ** (-0.5)
    spec = lambda third: pl.BlockSpec((1, rows, lanes), lambda b, p: (b, 0, third * pairs + p))
    return pl.pallas_call(
        functools.partial(self_forward_body, scaling=scaling, block=128),
        grid=(items, pairs),
        out_shape=[
            jax.ShapeDtypeStruct((items, rows, triple // 3), BF16),
            jax.ShapeDtypeStruct((items, heads, rows, 1), F32),
        ],
        in_specs=[spec(0), spec(1), spec(2)],
        out_specs=[spec(0), pl.BlockSpec((1, 2, rows, 1), lambda b, p: (b, p, 0, 0))],
        cost_estimate=pl.CostEstimate(
            flops=4 * items * rows * rows * triple // 3,
            bytes_accessed=items * rows * triple * 3,
            transcendentals=items * heads * rows * rows,
        ),
        name="self_attention",
    )(projected, projected, projected)


def self_backward_body(
    query_ref, key_ref, value_ref, grad_ref, lse_ref, query_out, key_out, value_out, *, scaling, block
):
    rows, lanes = query_ref.shape[1:]
    key_sum = [None] * (rows // block)
    value_sum = [None] * (rows // block)
    for start in range(0, rows, block):
        seen = start + block
        query_total = None
        for head in range(2):
            query = query_ref[0, start:seen]
            query = jnp.where(lanes_of(head, query.shape), query * scaling, 0).astype(BF16)
            grad = grad_ref[0, start:seen]
            grad = jnp.where(lanes_of(head, grad.shape), grad, 0).astype(BF16)
            key = key_ref[0, :seen]
            key_own = jnp.where(lanes_of(head, key.shape), key * scaling, 0).astype(BF16)
            scores = nt(query, key)
            row = lax.broadcasted_iota(jnp.int32, scores.shape, 0) + start
            column = lax.broadcasted_iota(jnp.int32, scores.shape, 1)
            scores = jnp.where(column <= row, scores, NEGATIVE)
            probability = jnp.exp(scores - lse_ref[0, head, start:seen])
            prob_grad = nt(grad, value_ref[0, :seen])
            weighted = probability * prob_grad
            centre = jnp.sum(weighted, axis=1, keepdims=True)
            score_grad = (weighted - probability * centre).astype(BF16)
            part = nn(score_grad, key_own)
            query_total = part if query_total is None else query_total + part
            key_part = tn(score_grad, query)
            value_part = tn(probability.astype(BF16), grad)
            for at in range(0, seen, block):
                k = at // block
                key_block = key_part[at : at + block]
                value_block = value_part[at : at + block]
                key_sum[k] = key_block if key_sum[k] is None else key_sum[k] + key_block
                value_sum[k] = value_block if value_sum[k] is None else value_sum[k] + value_block
        query_out[0, start:seen] = query_total.astype(BF16)
    for k in range(rows // block):
        key_out[0, k * block : (k + 1) * block] = key_sum[k].astype(BF16)
        value_out[0, k * block : (k + 1) * block] = value_sum[k].astype(BF16)


def self_attention_grads(projected, grad, lse):
    items, rows, triple = projected.shape
    heads = lse.shape[1]
    pairs = heads // 2
    lanes = triple // 3 // pairs
    scaling = (triple // 3 // heads) ** (-0.5)
    spec = lambda third: pl.BlockSpec((1, rows, lanes), lambda b, p: (b, 0, third * pairs + p))
    part = jax.ShapeDtypeStruct((items, rows, triple // 3), BF16)
    return pl.pallas_call(
        functools.partial(self_backward_body, scaling=scaling, block=128),
        grid=(items, pairs),
        out_shape=[part, part, part],
        in_specs=[
            spec(0),
            spec(1),
            spec(2),
            spec(0),
            pl.BlockSpec((1, 2, rows, 1), lambda b, p: (b, p, 0, 0)),
        ],
        out_specs=[spec(0)] * 3,
        cost_estimate=pl.CostEstimate(
            flops=10 * items * rows * rows * triple // 3,
            bytes_accessed=items * rows * triple * 6,
            transcendentals=items * heads * rows * rows,
        ),
        name="self_attention_grads",
    )(projected, projected, projected, grad, lse)


def cross_forward_body(length_ref, query_ref, key_ref, value_ref, out_ref, lse_ref, *, scaling):
    length = length_ref[pl.program_id(0)]
    total = None
    for head in range(2):
        query = query_ref[0]
        query = jnp.where(lanes_of(head, query.shape), query * scaling, 0).astype(BF16)
        scores = nt(query, key_ref[0])
        column = lax.broadcasted_iota(jnp.int32, scores.shape, 1)
        scores = jnp.where(column < length, scores, NEGATIVE)
        top = jnp.max(scores, axis=1, keepdims=True)
        weights = jnp.exp(scores - top)
        summed = jnp.sum(weights, axis=1, keepdims=True)
        probability = (weights * (1.0 / summed)).astype(BF16)
        value = value_ref[0]
        value = jnp.where(lanes_of(head, value.shape), value, 0).astype(BF16)
        part = nn(probability, value)
        total = part if total is None else total + part
        lse_ref[0, head] = top + jnp.log(summed)
    out_ref[0] = total.astype(BF16)


def cross_attention(lengths, query, key_value, heads):
    items, rows, width = query.shape
    text = key_value.shape[1]
    pairs = heads // 2
    lanes = width // pairs
    scaling = (width // heads) ** (-0.5)
    query_spec = pl.BlockSpec((1, rows, lanes), lambda b, p: (b, 0, p))
    return pl.pallas_call(
        functools.partial(cross_forward_body, scaling=scaling),
        grid=(items, pairs),
        out_shape=[
            jax.ShapeDtypeStruct((items, rows, width), BF16),
            jax.ShapeDtypeStruct((items, heads, rows, 1), F32),
        ],
        in_specs=[
            pl.BlockSpec(memory_space=pltpu.SMEM),
            query_spec,
            pl.BlockSpec((1, text, lanes), lambda b, p: (b, 0, p)),
            pl.BlockSpec((1, text, lanes), lambda b, p: (b, 0, pairs + p)),
        ],
        out_specs=[query_spec, pl.BlockSpec((1, 2, rows, 1), lambda b, p: (b, p, 0, 0))],
        cost_estimate=pl.CostEstimate(
            flops=4 * items * rows * text * width,
            bytes_accessed=items * rows * width * 6,
            transcendentals=items * heads * rows * text,
        ),
        name="cross_attention",
    )(lengths, query, key_value, key_value)


def cross_backward_body(
    length_ref, query_ref, key_ref, value_ref, grad_ref, lse_ref, query_out, key_out, value_out, *, scaling
):
    length = length_ref[pl.program_id(0)]
    query_total = key_total = value_total = None
    for head in range(2):
        query = query_ref[0]
        query = jnp.where(lanes_of(head, query.shape), query * scaling, 0).astype(BF16)
        grad = grad_ref[0]
        grad = jnp.where(lanes_of(head, grad.shape), grad, 0).astype(BF16)
        key = key_ref[0]
        key_own = jnp.where(lanes_of(head, key.shape), key * scaling, 0).astype(BF16)
        scores = nt(query, key)
        column = lax.broadcasted_iota(jnp.int32, scores.shape, 1)
        scores = jnp.where(column < length, scores, NEGATIVE)
        probability = jnp.exp(scores - lse_ref[0, head])
        prob_grad = nt(grad, value_ref[0])
        weighted = probability * prob_grad
        centre = jnp.sum(weighted, axis=1, keepdims=True)
        score_grad = (weighted - probability * centre).astype(BF16)
        parts = (
            nn(score_grad, key_own),
            tn(score_grad, query),
            tn(probability.astype(BF16), grad),
        )
        if head == 0:
            query_total, key_total, value_total = parts
        else:
            query_total, key_total, value_total = (
                query_total + parts[0],
                key_total + parts[1],
                value_total + parts[2],
            )
    query_out[0] = query_total.astype(BF16)
    key_out[0] = key_total.astype(BF16)
    value_out[0] = value_total.astype(BF16)


def cross_attention_grads(lengths, query, key_value, grad, lse):
    items, rows, width = query.shape
    text = key_value.shape[1]
    heads = lse.shape[1]
    pairs = heads // 2
    lanes = width // pairs
    scaling = (width // heads) ** (-0.5)
    query_spec = pl.BlockSpec((1, rows, lanes), lambda b, p: (b, 0, p))
    text_spec = pl.BlockSpec((1, text, lanes), lambda b, p: (b, 0, p))
    return pl.pallas_call(
        functools.partial(cross_backward_body, scaling=scaling),
        grid=(items, pairs),
        out_shape=[
            jax.ShapeDtypeStruct((items, rows, width), BF16),
            jax.ShapeDtypeStruct((items, text, width), BF16),
            jax.ShapeDtypeStruct((items, text, width), BF16),
        ],
        in_specs=[
            pl.BlockSpec(memory_space=pltpu.SMEM),
            query_spec,
            text_spec,
            pl.BlockSpec((1, text, lanes), lambda b, p: (b, 0, pairs + p)),
            query_spec,
            pl.BlockSpec((1, 2, rows, 1), lambda b, p: (b, p, 0, 0)),
        ],
        out_specs=[query_spec, text_spec, text_spec],
        cost_estimate=pl.CostEstimate(
            flops=10 * items * rows * text * width,
            bytes_accessed=items * rows * width * 10,
            transcendentals=items * heads * rows * text,
        ),
        name="cross_attention_grads",
    )(lengths, query, key_value, key_value, grad, lse)


def norm_forward(values, gain, bias):
    center = values - jnp.mean(values, axis=-1, keepdims=True)
    inverse = lax.rsqrt(jnp.mean(center * center, axis=-1, keepdims=True) + EPSILON)
    scaled = center * inverse
    normed = (scaled * gain.astype(F32) + bias.astype(F32)).astype(BF16)
    return normed, scaled, inverse


def norm_backward(upstream, scaled, inverse, gain):
    gain_grad = jnp.sum(upstream * scaled, axis=0)
    bias_grad = jnp.sum(upstream, axis=0)
    weighted = upstream * gain.astype(F32)
    input_grad = inverse * (
        weighted
        - jnp.mean(weighted, axis=-1, keepdims=True)
        - scaled * jnp.mean(weighted * scaled, axis=-1, keepdims=True)
    )
    return input_grad, gain_grad, bias_grad


def product(first, second):
    return jnp.dot(first, second, preferred_element_type=F32)


def weight_grad(inputs, grads):
    return jnp.einsum("sa,sb->ab", inputs, grads, preferred_element_type=F32).astype(BF16)


def input_grad_of(grads, weight):
    return jnp.einsum("sb,ab->sa", grads, weight, preferred_element_type=F32)


def gelu_parts(values):
    return jax.nn.gelu(values, approximate=True)


def per_device(
    tokens,
    text_states,
    caption_len,
    out_grad,
    norm1_gain,
    norm1_bias,
    qkv_weight,
    self_out,
    norm2_gain,
    norm2_bias,
    cross_query,
    cross_kv,
    cross_out,
    norm3_gain,
    norm3_bias,
    ff_in,
    ff_in_bias,
    ff_out,
    ff_out_bias,
):
    place = Place(lax.axis_size("dp") // 2, lax.axis_size("fsdp"))
    items, rows, width = tokens.shape
    text = text_states.shape[1]
    row_count = items * rows

    small = (
        norm1_gain, norm1_bias, norm2_gain, norm2_bias, norm3_gain, norm3_bias, ff_in_bias, ff_out_bias
    )
    sizes = [vector.shape[0] for vector in small]
    packed = jnp.concatenate(small)
    used = packed.shape[0]
    padded = -(-used // 128) * 128
    packed = jnp.pad(packed, (0, padded - used)).reshape(1, padded)
    spread = gather_small(place, packed)
    vectors, at = [], 0
    for size in sizes:
        vectors.append(spread[..., at : at + size].reshape(-1))
        at += size
    (n1_gain, n1_bias, n2_gain, n2_bias, n3_gain, n3_bias, in_bias, out_bias) = vectors

    ahead, behind = place.bits, place.bits[::-1]

    def whole(shard, order):
        return gather(place, shard, order).reshape(-1, shard.shape[1])

    w_qkv = whole(qkv_weight, ahead)
    w_self_out = whole(self_out, behind)
    w_cross_kv = whole(cross_kv, behind)
    w_cross_query = whole(cross_query, ahead)
    w_cross_out = whole(cross_out, behind)
    w_ff_in = whole(ff_in, ahead)
    w_ff_out = whole(ff_out, behind)

    token_values = tokens.reshape(row_count, width).astype(F32)
    text_rows = text_states.reshape(items * text, width)
    normed1, scaled1, inverse1 = norm_forward(token_values, n1_gain, n1_bias)
    projected = product(normed1, w_qkv).astype(BF16).reshape(items, rows, -1)
    attended1, lse1 = self_attention(projected, HEADS)
    attended1 = attended1.reshape(row_count, width)
    after_self = token_values + product(attended1, w_self_out)
    text_kv = product(text_rows, w_cross_kv).astype(BF16).reshape(items, text, -1)
    normed2, scaled2, inverse2 = norm_forward(after_self, n2_gain, n2_bias)
    query2 = product(normed2, w_cross_query).astype(BF16).reshape(items, rows, width)
    attended2, lse2 = cross_attention(caption_len, query2, text_kv, HEADS)
    attended2 = attended2.reshape(row_count, width)
    after_cross = after_self + product(attended2, w_cross_out)
    normed3, scaled3, inverse3 = norm_forward(after_cross, n3_gain, n3_bias)
    before = product(normed3, w_ff_in) + in_bias.astype(F32)
    middle = gelu_parts(before).astype(BF16)
    result = (after_cross + (product(middle, w_ff_out) + out_bias.astype(F32))).astype(BF16)

    cot = out_grad.reshape(row_count, width)
    cot_values = cot.astype(F32)
    ff_out_bias_grad = jnp.sum(cot_values, axis=0)
    ff_out_grad = scatter(place, weight_grad(middle, cot), behind, BF16)
    middle_grad = input_grad_of(cot, w_ff_out)
    before_grad = jax.vjp(gelu_parts, before)[1](middle_grad)[0].astype(BF16)
    ff_in_bias_grad = jnp.sum(before_grad.astype(F32), axis=0)
    ff_in_grad = scatter(place, weight_grad(normed3, before_grad), ahead, BF16)
    norm_input, n3_gain_grad, n3_bias_grad = norm_backward(
        input_grad_of(before_grad, w_ff_in), scaled3, inverse3, n3_gain
    )
    cross_grad = cot_values + norm_input
    cross_round = cross_grad.astype(BF16)
    cross_out_grad = scatter(place, weight_grad(attended2, cross_round), behind, BF16)
    attended2_grad = input_grad_of(cross_round, w_cross_out).astype(BF16)
    query2_grad, key2_grad, value2_grad = cross_attention_grads(
        caption_len, query2, text_kv, attended2_grad.reshape(items, rows, width), lse2
    )
    query2_grad = query2_grad.reshape(row_count, width)
    text_kv_grad = jnp.concatenate([key2_grad, value2_grad], axis=2).reshape(items * text, -1)
    cross_query_grad = scatter(place, weight_grad(normed2, query2_grad), ahead, BF16)
    cross_kv_grad = scatter(place, weight_grad(text_rows, text_kv_grad), behind, BF16)
    text_grad = input_grad_of(text_kv_grad, w_cross_kv).astype(BF16)
    norm_input, n2_gain_grad, n2_bias_grad = norm_backward(
        input_grad_of(query2_grad, w_cross_query), scaled2, inverse2, n2_gain
    )
    self_grad = cross_grad + norm_input
    self_round = self_grad.astype(BF16)
    self_out_grad = scatter(place, weight_grad(attended1, self_round), ahead, BF16)
    attended1_grad = input_grad_of(self_round, w_self_out).astype(BF16)
    parts = self_attention_grads(projected, attended1_grad.reshape(items, rows, width), lse1)
    projected_grad = jnp.concatenate(parts, axis=2).reshape(row_count, -1)
    qkv_weight_grad = scatter(place, weight_grad(normed1, projected_grad), behind, BF16)
    norm_input, n1_gain_grad, n1_bias_grad = norm_backward(
        input_grad_of(projected_grad, w_qkv), scaled1, inverse1, n1_gain
    )
    tokens_grad = (self_grad + norm_input).astype(BF16)

    small_grads = (
        n1_gain_grad, n1_bias_grad, n2_gain_grad, n2_bias_grad, n3_gain_grad, n3_bias_grad,
        ff_in_bias_grad, ff_out_bias_grad,
    )
    owners = place.lines * 2 * place.planes
    grads = jnp.concatenate([grad.reshape(owners, -1) for grad in small_grads], axis=1)
    grads = jnp.pad(grads, ((0, 0), (0, padded - used)))
    owned = scatter(place, grads, ahead, F32)[0]
    own, at = [], 0
    for size in sizes:
        own.append(owned[at : at + size])
        at += size
    return (
        result.reshape(items, rows, width),
        tokens_grad.reshape(items, rows, width),
        text_grad.reshape(items, text, width),
        own[0],
        own[1],
        qkv_weight_grad,
        self_out_grad,
        own[2],
        own[3],
        cross_query_grad,
        cross_kv_grad,
        cross_out_grad,
        own[4],
        own[5],
        ff_in_grad,
        own[6],
        ff_out_grad,
        own[7],
    )


def solution(mesh):
    whole = P(AXES, None, None)
    matrix = P(AXES, None)
    vector = P(AXES)
    weights = (
        vector, vector, matrix, matrix, vector, vector, matrix, matrix, matrix, vector, vector, matrix,
        vector, matrix, vector,
    )
    return jax.shard_map(
        per_device,
        mesh=mesh,
        in_specs=(whole, whole, vector, whole) + weights,
        out_specs=(whole, whole, whole) + weights,
        check_vma=False,
    )
```

time: 2100 us -> 862 us (0.41)
  waiting for transfers between devices: 1520 us -> 304 us
  Pallas kernels: 0 us -> 190 us
  blocking collectives: 150 us -> 0 us
  matrix products: 295 us -> 148 us
  starting transfers between devices: 0.73 us -> 136 us
  local copies, waits for them, and re-layouts: 71.4 us -> 35.9 us
    reduce_scatter x6 -> x0, waiting for transfers between devices: 1070 us -> none  [the longest x1 362 us: spread_grads(): lax.psum_scatter(totals[13], ('dp', 'fsdp'), scatter_dimension=0, tiled=T...]
    ppermute x0 -> x111, waiting for transfers between devices: none -> 304 us  [the longest x47 234 us: swap_plane(): lax.ppermute(value, AXES, self._pairs(lambda l, c, p: (l, c, p ^ bit)))]
    all_gather x7 -> x0, waiting for transfers between devices: 265 us -> none  [the longest x1 72.5 us: fetch_weights(): lax.all_gather(shards[11], ('dp', 'fsdp'), axis=0, tiled=True)]
    pallas_call x0 -> x25, Pallas kernels: none -> 190 us  [the longest x21 104 us: interleave(): pl.pallas_call(body, out_shape=jax.ShapeDtypeStruct((outer, count, rows,...]
    unnamed x15 -> x0, waiting for transfers between devices: 190 us -> none
    dot_general x66 -> x21, matrix products: 295 us -> 148 us  [the longest x7 51.7 us: input_grad_of(): return jnp.einsum('sb,ab->sa', grads, weight, preferred_element_type=F32)]
    ppermute x0 -> x111, starting transfers between devices: none -> 136 us  [the longest x48 83.5 us: shift_line(): lax.ppermute(value, AXES, self._pairs(lambda l, c, p: ((l + step) % self....]
    unnamed x2 -> x0, blocking collectives: 83.2 us -> none
  transfers between devices with their start and end apart: 14 -> 111, of which waited for: 11 -> 47; matrix products, arithmetic and copies ran while one was open for 13% -> 11% of each run, Pallas kernels for 0% -> 16%
where the time goes in v1:
time: 862 us; the launch traced here: 854 us
  waiting for transfers between devices  304 us (35%)
  Pallas kernels  190 us (22%)
  matrix products  148 us (17%)
  starting transfers between devices  136 us (16%)
  other arithmetic  37.5 us (4%)
  local copies, waits for them, and re-layouts  35.9 us (4%)
    ppermute x47, waiting for transfers between devices, swap_plane(): lax.ppermute(value, AXES, self._pairs(lambda l, c, p: (l, c, p ^ bit)))  234 us
    pallas_call x21, Pallas kernels, interleave(): pl.pallas_call(body, out_shape=jax.ShapeDtypeStruct((outer, count, rows,...  104 us
    ppermute x48, starting transfers between devices, shift_line(): lax.ppermute(value, AXES, self._pairs(lambda l, c, p: ((l + step) % self....  83.5 us
    ppermute x48, waiting for transfers between devices, shift_line(): lax.ppermute(value, AXES, self._pairs(lambda l, c, p: ((l + step) % self....  69.1 us
    dot_general x7, matrix products, input_grad_of(): return jnp.einsum('sb,ab->sa', grads, weight, preferred_element_type=F32)  51.7 us
    dot_general x7, matrix products, product(): return jnp.dot(first, second, preferred_element_type=F32)  50.8 us
    ppermute x47, starting transfers between devices, swap_plane(): lax.ppermute(value, AXES, self._pairs(lambda l, c, p: (l, c, p ^ bit)))  50.5 us
    dot_general x7, matrix products, weight_grad(): jnp.einsum('sa,sb->ab', inputs, grads, preferred_element_type=F32)  45.4 us
  transfers between devices with their start and end apart: 111, of which 47 were waited for; matrix products, arithmetic and copies ran while one was open for 11% of the time, Pallas kernels for 16%

profile of v1, /device:TPU:0, one launch (start us, length us, event | category | flops | bytes accessed | tf_op | source)
XLA Modules:
  0.0 854.0 jit_solution(5742751357634098989)
XLA Ops:
  0.7 5.5 concatenate.19
  6.2 5.1 collective-permute-start.2
  35.9 5.6 collective-permute-start.7
  45.4 5.9 collective-permute-start.28
  51.3 5.2 collective-permute-done.27
  56.4 5.4 collective-permute-start.48
  61.9 8.5 collective-permute-done.28
  80.2 16.9 %collective-permute-done.49 = bf16[128,1024]{1,0:T(8,128)(2,1)S(1)} collective-permute-done((bf16[128,1024]{1,0:T(8,128)(2,1)}, bf16[128,1024]{1,0:T(8,128)(2,1)S(1)}, u32[]{:S(2)}, u32[]{:S(2)}) %collective-permute-start.49) | collective-permute-done | bytes 262176 | tf_op jit(solution)/shard_map/ppermute | solution.py:43
  103.8 4.5 collective-permute-done.42
  129.5 40.5 %collective-permute-done.25.refs_3_ = bf16[4,32,1024]{2,1,0:T(8,128)(2,1)} collective-permute-done((bf16[4,32,1024]{2,1,0:T(8,128)(2,1)}, bf16[4,32,1024]{2,1,0:T(8,128)(2,1)}, u32[]{:S(2)}, u32[]{:S(2)}) %collective-permute-start.25) | collective-permute-done | bytes 262176 | tf_op jit(solution)/shard_map/ppermute | solution.py:48
  182.4 8.8 %interleave.22 = bf16[4,4,32,3072]{3,2,1,0:T(8,128)(2,1)} custom-call(s32[4]{0:T(128)} %broadcast_xor_fusion.1.slots_ref, bf16[4,32,3072]{2,1,0:T(8,128)(2,1)} %bitcast.501, bf16[4,32,3072]{2,1,0:T(8,128)(2,1)} %copy-done.29, bf16[4,32,3072]{2,1,0:T(8,128)(2,1)} %copy-done.30, bf16[4,32,3072]{2,1,0:T(8,128)(2,1)} %copy-done.31), custom_call_target="tpu_custom_call" | custom-call | tf_op jit(solution)/shard_map/interleave/pallas_call | solution.py:64
  192.7 43.0 %collective-permute-done.32.refs_3_ = bf16[4,32,2048]{2,1,0:T(8,128)(2,1)} collective-permute-done((bf16[4,32,2048]{2,1,0:T(8,128)(2,1)S(1)}, bf16[4,32,2048]{2,1,0:T(8,128)(2,1)}, u32[]{:S(2)}, u32[]{:S(2)}) %collective-permute-start.32) | collective-permute-done | bytes 524320 | tf_op jit(solution)/shard_map/ppermute | solution.py:48
  279.5 5.4 collective-permute-done.53.refs_3_
  284.9 5.4 interleave.40
  290.3 16.4 %collective-permute-done.46.refs_3_ = bf16[4,32,4096]{2,1,0:T(8,128)(2,1)} collective-permute-done((bf16[4,32,4096]{2,1,0:T(8,128)(2,1)}, bf16[4,32,4096]{2,1,0:T(8,128)(2,1)}, u32[]{:S(2)}, u32[]{:S(2)}) %collective-permute-start.46) | collective-permute-done | bytes 1048608 | tf_op jit(solution)/shard_map/ppermute | solution.py:48
  306.7 7.3 interleave.37
  314.0 5.3 interleave.32
  323.8 9.9 %interleave.23 = bf16[4,2,128,3072]{3,2,1,0:T(8,128)(2,1)} custom-call(s32[2]{0:T(128)} %iota_xor_fusion.slots_ref, bf16[4,128,3072]{2,1,0:T(8,128)(2,1)} %bitcast.440, bf16[4,128,3072]{2,1,0:T(8,128)(2,1)} %collective-permute-done.12.refs_1_), custom_call_target="tpu_custom_call" | custom-call | tf_op jit(solution)/shard_map/interleave/pallas_call | solution.py:64
  333.7 9.1 %convolution_convert_fusion.2 = bf16[768,3072]{1,0:T(8,128)(2,1)} fusion(bf16[768,1024]{1,0:T(8,128)(2,1)} %bitcast.517, bf16[1024,3072]{1,0:T(8,128)(2,1)} %bitcast.463), kind=kOutput, calls=%fused_computation.30 | convolution fusion | flops 4834197504 | bytes 12582912 | tf_op jit(solution)/shard_map/dot_general | solution.py:419
  342.8 23.4 %self_attention.1 = (bf16[2,384,1024]{2,1,0:T(8,128)(2,1)}, f32[2,16,384,1]{3,2,1,0:T(8,128)}) custom-call(bf16[2,384,3072]{2,1,0:T(8,128)(2,1)} %bitcast.417, bf16[2,384,3072]{2,1,0:T(8,128)(2,1)} %bitcast.418, bf16[2,384,3072]{2,1,0:T(8,128)(2,1)} %bitcast.419), custom_call_target="tpu_custom_call" | custom-call | flops 1207959552 | bytes 7077888 | tf_op jit(solution)/shard_map/self_attention/pallas_call | solution.py:186
  375.9 14.7 %cross_attention.1 = (bf16[2,384,1024]{2,1,0:T(8,128)(2,1)}, f32[2,16,384,1]{3,2,1,0:T(8,128)}) custom-call(s32[2]{0:T(128)} %length_ref.3, bf16[2,384,1024]{2,1,0:T(8,128)(2,1)} %bitcast.473, bf16[2,128,2048]{2,1,0:T(8,128)(2,1)} %bitcast.435, bf16[2,128,2048]{2,1,0:T(8,128)(2,1)} %bitcast.436), custom_call_target="tpu_custom_call" | custom-call | flops 402653184 | bytes 4718592 | tf_op jit(solution)/shard_map/cross_attention/pallas_call | solution.py:302
  397.0 9.6 %interleave.38 = bf16[4,2,128,4096]{3,2,1,0:T(8,128)(2,1)} custom-call(s32[2]{0:T(128)} %iota_xor_fusion.slots_ref, bf16[4,128,4096]{2,1,0:T(8,128)(2,1)} %bitcast.434, bf16[4,128,4096]{2,1,0:T(8,128)(2,1)} %collective-permute-done.47.refs_1_), custom_call_target="tpu_custom_call" | custom-call | tf_op jit(solution)/shard_map/interleave/pallas_call | solution.py:64
  406.7 13.7 %fusion.81 = f32[768,4096]{1,0:T(8,128)} fusion(bf16[1024,4096]{1,0:T(8,128)(2,1)} %bitcast.448, f32[768,1024]{1,0:T(8,128)} %copy-done.4, f32[1024]{0:T(1024)S(1)} %reshape.638, f32[1024]{0:T(1024)S(1)} %reshape.637, f32[768]{0:T(1024)S(1)} %add_rsqrt_fusion, f32[768]{0:T(1024)S(1)} %broadcast_multiply_fusion.6), kind=kOutput, calls=%fused_computation.267 | convolution fusion | flops 6446383104 | bytes 24131584 | tf_op jit(solution)/shard_map/dot_general | solution.py:419
  420.4 7.8 interleave.41
  428.2 18.3 %convert_reduce_fusion = (f32[4096]{0:T(1024)S(1)}, bf16[768,4096]{1,0:T(8,128)(2,1)S(1)}) fusion(f32[768,4096]{1,0:T(8,128)} %fusion.81, f32[4096]{0:T(1024)S(1)} %bitcast.563, bf16[4096,1024]{1,0:T(8,128)(2,1)} %bitcast.444, bf16[768,1024]{1,0:T(8,128)(2,1)S(1)} %bitcast.467), kind=kOutput, calls=%fused_computation.19 | convolution fusion | flops 6514798592 | bytes 28868608 | tf_op jit(solution)/shard_map/sb,ab->sa/dot_general | solution.py:427
  446.5 12.5 %multiply_reduce_fusion = (f32[1024]{0:T(1024)S(1)}, f32[768]{0:T(1024)S(1)}, f32[768]{0:T(1024)S(1)}, f32[1024]{0:T(1024)S(1)}, f32[768,1024]{1,0:T(8,128)S(1)}) fusion(f32[768,1024]{1,0:T(8,128)S(1)} %copy-done.5, f32[768]{0:T(1024)S(1)} %add_rsqrt_fusion, f32[768]{0:T(1024)S(1)} %broadcast_multiply_fusion.6, f32[1024]{0:T(1024)S(1)} %reshape.637, ...), kind=kOutput, calls=%fused_computation.57 | convolution fusion | flops 6449524736 | bytes 20996096 | tf_op jit(solution)/shard_map/sb,ab->sa/dot_general | solution.py:427
  463.7 17.4 %cross_attention_grads.1 = (bf16[2,384,1024]{2,1,0:T(8,128)(2,1)}, bf16[2,128,1024]{2,1,0:T(8,128)(2,1)}, bf16[2,128,1024]{2,1,0:T(8,128)(2,1)}) custom-call(s32[2]{0:T(128)} %length_ref.3, bf16[2,384,1024]{2,1,0:T(8,128)(2,1)} %bitcast.474, bf16[2,128,2048]{2,1,0:T(8,128)(2,1)} %bitcast.437, bf16[2,128,2048]{2,1,0:T(8,128)(2,1)} %bitcast.438, ...), custom_call_target="tpu_custom_call" | custom-call | flops 1006632960 | bytes 7864320 | tf_op jit(solution)/shard_map/cross_attention_grads/pallas_call | solution.py:372
  481.0 5.5 multiply_reduce_fusion.1
  501.0 9.8 %convolution_convert_fusion.1 = bf16[1024,4096]{1,0:T(8,128)(2,1)} fusion(bf16[768,4096]{1,0:T(8,128)(2,1)S(1)} %bitcast.580, f32[768,1024]{1,0:T(8,128)S(1)} %copy-done.6, f32[1024]{0:T(1024)S(1)} %reshape.638, f32[1024]{0:T(1024)S(1)} %reshape.637, f32[768]{0:T(1024)S(1)} %add_rsqrt_fusion, f32[768]{0:T(1024)S(1)} %broadcast_multiply_fusion.6), kind=kOutput, calls=%fused_computation.27 | convolution fusion | flops 6450577408 | bytes 17840128 | tf_op jit(solution)/shard_map/sa,sb->ab/dot_general | solution.py:423
  510.9 14.9 %convolution_convert_fusion = bf16[4096,1024]{1,0:T(8,128)(2,1)} fusion(bf16[768,1024]{1,0:T(8,128)(2,1)S(1)} %bitcast.468, f32[768,4096]{1,0:T(8,128)} %fusion.81, f32[4096]{0:T(1024)S(1)} %bitcast.564), kind=kOutput, calls=%fused_computation.26 | convolution fusion | flops 6478102528 | bytes 22560768 | tf_op jit(solution)/shard_map/sa,sb->ab/dot_general | solution.py:423
  525.8 12.4 %add_convert_fusion = bf16[768,1024]{1,0:T(8,128)(2,1)} fusion(f32[768,1024]{1,0:T(8,128)S(1)} %copy-done.6, bf16[4096,1024]{1,0:T(8,128)(2,1)S(1)} %bitcast.447, f32[1024]{0:T(1024)S(1)} %copy-done.61, f32[768,4096]{1,0:T(8,128)} %fusion.81, f32[4096]{0:T(1024)S(1)} %bitcast.565), kind=kOutput, calls=%fused_computation.63 | convolution fusion | flops 6476267520 | bytes 25710592 | tf_op jit(solution)/shard_map/dot_general | solution.py:419
  538.2 31.2 %self_attention_grads.1 = (bf16[2,384,1024]{2,1,0:T(8,128)(2,1)}, bf16[2,384,1024]{2,1,0:T(8,128)(2,1)}, bf16[2,384,1024]{2,1,0:T(8,128)(2,1)}) custom-call(bf16[2,384,3072]{2,1,0:T(8,128)(2,1)} %bitcast.420, bf16[2,384,3072]{2,1,0:T(8,128)(2,1)} %bitcast.421, bf16[2,384,3072]{2,1,0:T(8,128)(2,1)} %bitcast.422, bf16[2,384,1024]{2,1,0:T(8,128)(2,1)} %bitcast.520, ...), custom_call_target="tpu_custom_call" | custom-call | flops 3019898880 | bytes 14155776 | tf_op jit(solution)/shard_map/self_attention_grads/pallas_call | solution.py:253
  572.8 7.5 bitcast_convert_fusion
  580.4 7.3 fusion.29
  597.4 5.3 dynamic-slice_bitcast_fusion.1
  614.4 13.4 %collective-permute-start.61 = (f32[1,384]{1,0:T(1,128)S(1)}, f32[1,384]{1,0:T(1,128)S(1)}, u32[]{:S(2)}, u32[]{:S(2)}) collective-permute-start(f32[1,384]{1,0:T(1,128)S(1)} %get-tuple-element.95), channel_id=1, source_target_pairs={{0,24},{1,25},{2,26},{3,27},{4,28},{5,29},{6,30},{7,31},{8,0},{9,1... | collective-permute-start | bytes 4616 | tf_op jit(solution)/shard_map/ppermute | solution.py:43
  644.9 10.0 %collective-permute-done.78 = bf16[4,32,1024]{2,1,0:T(8,128)(2,1)S(1)} collective-permute-done((bf16[4,32,1024]{2,1,0:T(8,128)(2,1)S(1)}, bf16[4,32,1024]{2,1,0:T(8,128)(2,1)S(1)}, u32[]{:S(2)}, u32[]{:S(2)}) %collective-permute-start.78) | collective-permute-done | bytes 262176 | tf_op jit(solution)/shard_map/ppermute | solution.py:48
  658.7 5.4 collective-permute-done.72
  701.8 9.9 %collective-permute-done.84 = bf16[4,32,2048]{2,1,0:T(8,128)(2,1)S(1)} collective-permute-done((bf16[4,32,2048]{2,1,0:T(8,128)(2,1)S(1)}, bf16[4,32,2048]{2,1,0:T(8,128)(2,1)S(1)}, u32[]{:S(2)}, u32[]{:S(2)}) %collective-permute-start.84) | collective-permute-done | bytes 524320 | tf_op jit(solution)/shard_map/ppermute | solution.py:48
  715.5 13.1 %collective-permute-done.64 = bf16[4,32,3072]{2,1,0:T(8,128)(2,1)S(1)} collective-permute-done((bf16[4,32,3072]{2,1,0:T(8,128)(2,1)S(1)}, bf16[4,32,3072]{2,1,0:T(8,128)(2,1)S(1)}, u32[]{:S(2)}, u32[]{:S(2)}) %collective-permute-start.64) | collective-permute-done | bytes 786464 | tf_op jit(solution)/shard_map/ppermute | solution.py:48
  733.6 5.0 fusion.11
  745.5 13.8 %collective-permute-done.65 = bf16[4,32,3072]{2,1,0:T(8,128)(2,1)} collective-permute-done((bf16[4,32,3072]{2,1,0:T(8,128)(2,1)S(1)}, bf16[4,32,3072]{2,1,0:T(8,128)(2,1)}, u32[]{:S(2)}, u32[]{:S(2)}) %collective-permute-start.65) | collective-permute-done | bytes 786464 | tf_op jit(solution)/shard_map/ppermute | solution.py:48
  762.5 19.1 %collective-permute-done.99 = bf16[4,32,4096]{2,1,0:T(8,128)(2,1)S(1)} collective-permute-done((bf16[4,32,4096]{2,1,0:T(8,128)(2,1)S(1)}, bf16[4,32,4096]{2,1,0:T(8,128)(2,1)S(1)}, u32[]{:S(2)}, u32[]{:S(2)}) %collective-permute-start.99) | collective-permute-done | bytes 1048608 | tf_op jit(solution)/shard_map/ppermute | solution.py:48
  789.9 5.2 collective-permute-done.67
  797.4 13.1 %collective-permute-done.106 = bf16[4,128,1024]{2,1,0:T(8,128)(2,1)S(1)} collective-permute-done((bf16[4,128,1024]{2,1,0:T(8,128)(2,1)S(1)}, bf16[4,128,1024]{2,1,0:T(8,128)(2,1)S(1)}, u32[]{:S(2)}, u32[]{:S(2)}) %collective-permute-start.106) | collective-permute-done | bytes 1048608 | tf_op jit(solution)/shard_map/ppermute | solution.py:48
  812.5 12.7 %collective-permute-done.100 = bf16[4,32,4096]{2,1,0:T(8,128)(2,1)S(1)} collective-permute-done((bf16[4,32,4096]{2,1,0:T(8,128)(2,1)S(1)}, bf16[4,32,4096]{2,1,0:T(8,128)(2,1)S(1)}, u32[]{:S(2)}, u32[]{:S(2)}) %collective-permute-start.100) | collective-permute-done | bytes 1048608 | tf_op jit(solution)/shard_map/ppermute | solution.py:48
  827.9 8.6 %collective-permute-done.105 = bf16[4,128,1024]{2,1,0:T(8,128)(2,1)S(1)} collective-permute-done((bf16[4,128,1024]{2,1,0:T(8,128)(2,1)S(1)}, bf16[4,128,1024]{2,1,0:T(8,128)(2,1)S(1)}, u32[]{:S(2)}, u32[]{:S(2)}) %collective-permute-start.105) | collective-permute-done | bytes 1048608 | tf_op jit(solution)/shard_map/ppermute | solution.py:48
  844.5 8.4 collective-permute-done.109
  (521 shorter events, 289.1 us)
Async XLA Ops:
  35.5 34.9 %collective-permute-start.6 = (bf16[32,3072]{1,0:T(8,128)(2,1)}, bf16[32,3072]{1,0:T(8,128)(2,1)S(1)}, u32[]{:S(2)}, u32[]{:S(2)}) collective-permute-start(bf16[32,3072]{1,0:T(8,128)(2,1)} %param.40), channel_id=1, source_target_pairs={{0,8},{1,9},{2,10},{3,11},{4,12},{5,13},{6,14},{7,15},{8,16},{9,17... | collective-permute-start | bytes 589832 | tf_op jit(solution)/shard_map/ppermute | solution.py:43
  35.9 34.6 %collective-permute-start.7 = (bf16[32,3072]{1,0:T(8,128)(2,1)}, bf16[32,3072]{1,0:T(8,128)(2,1)S(1)}, u32[]{:S(2)}, u32[]{:S(2)}) collective-permute-start(bf16[32,3072]{1,0:T(8,128)(2,1)} %param.40), channel_id=1, source_target_pairs={{0,16},{1,17},{2,18},{3,19},{4,20},{5,21},{6,22},{7,23},{8,24},{9,... | collective-permute-start | bytes 589832 | tf_op jit(solution)/shard_map/ppermute | solution.py:43
  41.5 33.3 %collective-permute-start.8 = (bf16[32,3072]{1,0:T(8,128)(2,1)}, bf16[32,3072]{1,0:T(8,128)(2,1)S(1)}, u32[]{:S(2)}, u32[]{:S(2)}) collective-permute-start(bf16[32,3072]{1,0:T(8,128)(2,1)} %param.40), channel_id=1, source_target_pairs={{0,24},{1,25},{2,26},{3,27},{4,28},{5,29},{6,30},{7,31},{8,0},{9,1... | collective-permute-start | bytes 589832 | tf_op jit(solution)/shard_map/ppermute | solution.py:43
  45.4 25.0 %collective-permute-start.28 = (bf16[32,2048]{1,0:T(8,128)(2,1)}, bf16[32,2048]{1,0:T(8,128)(2,1)S(1)}, u32[]{:S(2)}, u32[]{:S(2)}) collective-permute-start(bf16[32,2048]{1,0:T(8,128)(2,1)} %param.45), channel_id=1, source_target_pairs={{0,16},{1,17},{2,18},{3,19},{4,20},{5,21},{6,22},{7,23},{8,24},{9,... | collective-permute-start | bytes 393224 | tf_op jit(solution)/shard_map/ppermute | solution.py:43
  56.4 23.2 %collective-permute-start.48 = (bf16[128,1024]{1,0:T(8,128)(2,1)}, bf16[128,1024]{1,0:T(8,128)(2,1)S(1)}, u32[]{:S(2)}, u32[]{:S(2)}) collective-permute-start(bf16[128,1024]{1,0:T(8,128)(2,1)} %param.51), channel_id=1, source_target_pairs={{0,8},{1,9},{2,10},{3,11},{4,12},{5,13},{6,14},{7,15},{8,16},{9,17... | collective-permute-start | bytes 786440 | tf_op jit(solution)/shard_map/ppermute | solution.py:43
  70.4 26.6 %collective-permute-start.49 = (bf16[128,1024]{1,0:T(8,128)(2,1)}, bf16[128,1024]{1,0:T(8,128)(2,1)S(1)}, u32[]{:S(2)}, u32[]{:S(2)}) collective-permute-start(bf16[128,1024]{1,0:T(8,128)(2,1)} %param.51), channel_id=1, source_target_pairs={{0,16},{1,17},{2,18},{3,19},{4,20},{5,21},{6,22},{7,23},{8,24},{9,... | collective-permute-start | bytes 786440 | tf_op jit(solution)/shard_map/ppermute | solution.py:43
  70.5 28.9 %collective-permute-start.50 = (bf16[128,1024]{1,0:T(8,128)(2,1)}, bf16[128,1024]{1,0:T(8,128)(2,1)S(1)}, u32[]{:S(2)}, u32[]{:S(2)}) collective-permute-start(bf16[128,1024]{1,0:T(8,128)(2,1)} %param.51), channel_id=1, source_target_pairs={{0,24},{1,25},{2,26},{3,27},{4,28},{5,29},{6,30},{7,31},{8,0},{9,1... | collective-permute-start | bytes 786440 | tf_op jit(solution)/shard_map/ppermute | solution.py:43
  74.8 26.1 %collective-permute-start.41 = (bf16[32,4096]{1,0:T(8,128)(2,1)}, bf16[32,4096]{1,0:T(8,128)(2,1)S(1)}, u32[]{:S(2)}, u32[]{:S(2)}) collective-permute-start(bf16[32,4096]{1,0:T(8,128)(2,1)} %param.49), channel_id=1, source_target_pairs={{0,8},{1,9},{2,10},{3,11},{4,12},{5,13},{6,14},{7,15},{8,16},{9,17... | collective-permute-start | bytes 786440 | tf_op jit(solution)/shard_map/ppermute | solution.py:43
  79.0 46.6 %collective-permute-start.9 = (bf16[4,32,3072]{2,1,0:T(8,128)(2,1)}, bf16[4,32,3072]{2,1,0:T(8,128)(2,1)S(1)}, u32[]{:S(2)}, u32[]{:S(2)}) collective-permute-start(bf16[4,32,3072]{2,1,0:T(8,128)(2,1)} %bitcast.499), channel_id=1, source_target_pairs={{0,1},{1,0},{2,3},{3,2},{4,5},{5,4},{6,7},{7,6},{8,9},{9,8},{10,11... | collective-permute-start | bytes 2359304 | tf_op jit(solution)/shard_map/ppermute | solution.py:48
  79.6 28.7 %collective-permute-start.42 = (bf16[32,4096]{1,0:T(8,128)(2,1)}, bf16[32,4096]{1,0:T(8,128)(2,1)S(1)}, u32[]{:S(2)}, u32[]{:S(2)}) collective-permute-start(bf16[32,4096]{1,0:T(8,128)(2,1)} %param.49), channel_id=1, source_target_pairs={{0,16},{1,17},{2,18},{3,19},{4,20},{5,21},{6,22},{7,23},{8,24},{9,... | collective-permute-start | bytes 786440 | tf_op jit(solution)/shard_map/ppermute | solution.py:43
  113.4 65.7 %collective-permute-start.10 = (bf16[4,32,3072]{2,1,0:T(8,128)(2,1)}, bf16[4,32,3072]{2,1,0:T(8,128)(2,1)S(1)}, u32[]{:S(2)}, u32[]{:S(2)}) collective-permute-start(bf16[4,32,3072]{2,1,0:T(8,128)(2,1)} %bitcast.500), channel_id=1, source_target_pairs={{0,2},{1,3},{2,0},{3,1},{4,6},{5,7},{6,4},{7,5},{8,10},{9,11},{10,... | collective-permute-start | bytes 2359304 | tf_op jit(solution)/shard_map/ppermute | solution.py:48
  124.1 54.0 %collective-permute-start.30 = (bf16[4,32,2048]{2,1,0:T(8,128)(2,1)}, bf16[4,32,2048]{2,1,0:T(8,128)(2,1)S(1)}, u32[]{:S(2)}, u32[]{:S(2)}) collective-permute-start(bf16[4,32,2048]{2,1,0:T(8,128)(2,1)} %bitcast.508), channel_id=1, source_target_pairs={{0,2},{1,3},{2,0},{3,1},{4,6},{5,7},{6,4},{7,5},{8,10},{9,11},{10,... | collective-permute-start | bytes 1572872 | tf_op jit(solution)/shard_map/ppermute | solution.py:48
  125.7 55.3 %collective-permute-start.11 = (bf16[4,32,3072]{2,1,0:T(8,128)(2,1)S(1)}, bf16[4,32,3072]{2,1,0:T(8,128)(2,1)S(1)}, u32[]{:S(2)}, u32[]{:S(2)}) collective-permute-start(bf16[4,32,3072]{2,1,0:T(8,128)(2,1)S(1)} %collective-permute-done.9.refs_1_), channel_id=1, source_target_pairs={{0,2},{1,3},{2,0},{3,1},{4,6},{5,7},{6,4},{7,5},{8,10},{9,11},{10,... | collective-permute-start | bytes 2359304 | tf_op jit(solution)/shard_map/ppermute | solution.py:48
  126.3 43.7 %collective-permute-start.25 = (bf16[4,32,1024]{2,1,0:T(8,128)(2,1)}, bf16[4,32,1024]{2,1,0:T(8,128)(2,1)}, u32[]{:S(2)}, u32[]{:S(2)}) collective-permute-start(bf16[4,32,1024]{2,1,0:T(8,128)(2,1)} %copy-done.36), channel_id=1, source_target_pairs={{0,2},{1,3},{2,0},{3,1},{4,6},{5,7},{6,4},{7,5},{8,10},{9,11},{10,... | collective-permute-start | bytes 786440 | tf_op jit(solution)/shard_map/ppermute | solution.py:48
  129.2 44.9 %collective-permute-start.39 = (bf16[4,32,1024]{2,1,0:T(8,128)(2,1)}, bf16[4,32,1024]{2,1,0:T(8,128)(2,1)}, u32[]{:S(2)}, u32[]{:S(2)}) collective-permute-start(bf16[4,32,1024]{2,1,0:T(8,128)(2,1)} %copy-done.38), channel_id=1, source_target_pairs={{0,1},{1,0},{2,3},{3,2},{4,5},{5,4},{6,7},{7,6},{8,9},{9,8},{10,11... | collective-permute-start | bytes 786440 | tf_op jit(solution)/shard_map/ppermute | solution.py:48
  170.0 21.3 %collective-permute-start.31 = (bf16[4,32,2048]{2,1,0:T(8,128)(2,1)}, bf16[4,32,2048]{2,1,0:T(8,128)(2,1)}, u32[]{:S(2)}, u32[]{:S(2)}) collective-permute-start(bf16[4,32,2048]{2,1,0:T(8,128)(2,1)} %bitcast.509), channel_id=1, source_target_pairs={{0,1},{1,0},{2,3},{3,2},{4,5},{5,4},{6,7},{7,6},{8,9},{9,8},{10,11... | collective-permute-start | bytes 1572872 | tf_op jit(solution)/shard_map/ppermute | solution.py:48
  174.0 79.4 %collective-permute-start.51 = (bf16[4,128,1024]{2,1,0:T(8,128)(2,1)}, bf16[4,128,1024]{2,1,0:T(8,128)(2,1)}, u32[]{:S(2)}, u32[]{:S(2)}) collective-permute-start(bf16[4,128,1024]{2,1,0:T(8,128)(2,1)} %bitcast.478), channel_id=1, source_target_pairs={{0,2},{1,3},{2,0},{3,1},{4,6},{5,7},{6,4},{7,5},{8,10},{9,11},{10,... | collective-permute-start | bytes 3145736 | tf_op jit(solution)/shard_map/ppermute | solution.py:48
  178.1 75.4 %collective-permute-start.52 = (bf16[4,128,1024]{2,1,0:T(8,128)(2,1)}, bf16[4,128,1024]{2,1,0:T(8,128)(2,1)}, u32[]{:S(2)}, u32[]{:S(2)}) collective-permute-start(bf16[4,128,1024]{2,1,0:T(8,128)(2,1)} %bitcast.479), channel_id=1, source_target_pairs={{0,1},{1,0},{2,3},{3,2},{4,5},{5,4},{6,7},{7,6},{8,9},{9,8},{10,11... | collective-permute-start | bytes 3145736 | tf_op jit(solution)/shard_map/ppermute | solution.py:48
  179.1 74.8 %collective-permute-start.44 = (bf16[4,32,4096]{2,1,0:T(8,128)(2,1)}, bf16[4,32,4096]{2,1,0:T(8,128)(2,1)}, u32[]{:S(2)}, u32[]{:S(2)}) collective-permute-start(bf16[4,32,4096]{2,1,0:T(8,128)(2,1)} %bitcast.475), channel_id=1, source_target_pairs={{0,1},{1,0},{2,3},{3,2},{4,5},{5,4},{6,7},{7,6},{8,9},{9,8},{10,11... | collective-permute-start | bytes 3145736 | tf_op jit(solution)/shard_map/ppermute | solution.py:48
  180.9 54.8 %collective-permute-start.32 = (bf16[4,32,2048]{2,1,0:T(8,128)(2,1)S(1)}, bf16[4,32,2048]{2,1,0:T(8,128)(2,1)}, u32[]{:S(2)}, u32[]{:S(2)}) collective-permute-start(bf16[4,32,2048]{2,1,0:T(8,128)(2,1)S(1)} %collective-permute-done.30.refs_1_), channel_id=1, source_target_pairs={{0,1},{1,0},{2,3},{3,2},{4,5},{5,4},{6,7},{7,6},{8,9},{9,8},{10,11... | collective-permute-start | bytes 1572872 | tf_op jit(solution)/shard_map/ppermute | solution.py:48
  191.3 132.6 %collective-permute-start.12 = (bf16[4,128,3072]{2,1,0:T(8,128)(2,1)}, bf16[4,128,3072]{2,1,0:T(8,128)(2,1)}, u32[]{:S(2)}, u32[]{:S(2)}) collective-permute-start(bf16[4,128,3072]{2,1,0:T(8,128)(2,1)} %bitcast.439), channel_id=1, source_target_pairs={{0,4},{1,5},{2,6},{3,7},{4,0},{5,1},{6,2},{7,3},{8,12},{9,13},{10,... | collective-permute-start | bytes 9437192 | tf_op jit(solution)/shard_map/ppermute | solution.py:51
  235.7 17.2 %collective-permute-start.5 = (bf16[4,4,1,384]{3,1,0,2:T(4,128)(2,1)S(1)}, bf16[4,4,1,384]{3,1,0,2:T(4,128)(2,1)S(1)}, u32[]{:S(2)}, u32[]{:S(2)}) collective-permute-start(bf16[4,4,1,384]{3,1,0,2:T(4,128)(2,1)S(1)} %bitcast.558), channel_id=1, source_target_pairs={{0,4},{1,5},{2,6},{3,7},{4,0},{5,1},{6,2},{7,3},{8,12},{9,13},{10,... | collective-permute-start | bytes 36872 | tf_op jit(solution)/shard_map/ppermute | solution.py:51
  254.0 60.1 %collective-permute-start.33 = (bf16[4,128,2048]{2,1,0:T(8,128)(2,1)}, bf16[4,128,2048]{2,1,0:T(8,128)(2,1)}, u32[]{:S(2)}, u32[]{:S(2)}) collective-permute-start(bf16[4,128,2048]{2,1,0:T(8,128)(2,1)} %bitcast.461), channel_id=1, source_target_pairs={{0,4},{1,5},{2,6},{3,7},{4,0},{5,1},{6,2},{7,3},{8,12},{9,13},{10,... | collective-permute-start | bytes 6291464 | tf_op jit(solution)/shard_map/ppermute | solution.py:51
  258.6 31.7 %collective-permute-start.45 = (bf16[4,32,4096]{2,1,0:T(8,128)(2,1)S(1)}, bf16[4,32,4096]{2,1,0:T(8,128)(2,1)}, u32[]{:S(2)}, u32[]{:S(2)}) collective-permute-start(bf16[4,32,4096]{2,1,0:T(8,128)(2,1)S(1)} %bitcast.477), channel_id=1, source_target_pairs={{0,2},{1,3},{2,0},{3,1},{4,6},{5,7},{6,4},{7,5},{8,10},{9,11},{10,... | collective-permute-start | bytes 3145736 | tf_op jit(solution)/shard_map/ppermute | solution.py:48
  259.4 25.5 %collective-permute-start.53 = (bf16[4,128,1024]{2,1,0:T(8,128)(2,1)}, bf16[4,128,1024]{2,1,0:T(8,128)(2,1)}, u32[]{:S(2)}, u32[]{:S(2)}) collective-permute-start(bf16[4,128,1024]{2,1,0:T(8,128)(2,1)} %collective-permute-done.51.refs_1_), channel_id=1, source_target_pairs={{0,1},{1,0},{2,3},{3,2},{4,5},{5,4},{6,7},{7,6},{8,9},{9,8},{10,11... | collective-permute-start | bytes 3145736 | tf_op jit(solution)/shard_map/ppermute | solution.py:48
  260.5 46.2 %collective-permute-start.46 = (bf16[4,32,4096]{2,1,0:T(8,128)(2,1)}, bf16[4,32,4096]{2,1,0:T(8,128)(2,1)}, u32[]{:S(2)}, u32[]{:S(2)}) collective-permute-start(bf16[4,32,4096]{2,1,0:T(8,128)(2,1)} %collective-permute-done.44.refs_1_), channel_id=1, source_target_pairs={{0,2},{1,3},{2,0},{3,1},{4,6},{5,7},{6,4},{7,5},{8,10},{9,11},{10,... | collective-permute-start | bytes 3145736 | tf_op jit(solution)/shard_map/ppermute | solution.py:48
  290.3 130.1 %collective-permute-start.54 = (bf16[4,512,1024]{2,1,0:T(8,128)(2,1)}, bf16[4,512,1024]{2,1,0:T(8,128)(2,1)}, u32[]{:S(2)}, u32[]{:S(2)}) collective-permute-start(bf16[4,512,1024]{2,1,0:T(8,128)(2,1)} %bitcast.431), channel_id=1, source_target_pairs={{0,4},{1,5},{2,6},{3,7},{4,0},{5,1},{6,2},{7,3},{8,12},{9,13},{10,... | collective-permute-start | bytes 12582920 | tf_op jit(solution)/shard_map/ppermute | solution.py:51
  314.0 83.0 %collective-permute-start.47 = (bf16[4,128,4096]{2,1,0:T(8,128)(2,1)}, bf16[4,128,4096]{2,1,0:T(8,128)(2,1)}, u32[]{:S(2)}, u32[]{:S(2)}) collective-permute-start(bf16[4,128,4096]{2,1,0:T(8,128)(2,1)} %bitcast.433), channel_id=1, source_target_pairs={{0,4},{1,5},{2,6},{3,7},{4,0},{5,1},{6,2},{7,3},{8,12},{9,13},{10,... | collective-permute-start | bytes 12582920 | tf_op jit(solution)/shard_map/ppermute | solution.py:51
  596.6 97.0 %collective-permute-start.62 = (bf16[4,128,3072]{2,1,0:T(8,128)(2,1)S(1)}, bf16[4,128,3072]{2,1,0:T(8,128)(2,1)S(1)}, u32[]{:S(2)}, u32[]{:S(2)}) collective-permute-start(bf16[4,128,3072]{2,1,0:T(8,128)(2,1)S(1)} %dynamic-slice_bitcast_fusion.2), channel_id=1, source_target_pairs={{0,4},{1,5},{2,6},{3,7},{4,0},{5,1},{6,2},{7,3},{8,12},{9,13},{10,... | collective-permute-start | bytes 9437192 | tf_op jit(solution)/shard_map/ppermute | solution.py:51
  597.0 37.4 %collective-permute-start.69 = (bf16[4,128,1024]{2,1,0:T(8,128)(2,1)S(1)}, bf16[4,128,1024]{2,1,0:T(8,128)(2,1)S(1)}, u32[]{:S(2)}, u32[]{:S(2)}) collective-permute-start(bf16[4,128,1024]{2,1,0:T(8,128)(2,1)S(1)} %dynamic-slice_bitcast_fusion.10), channel_id=1, source_target_pairs={{0,4},{1,5},{2,6},{3,7},{4,0},{5,1},{6,2},{7,3},{8,12},{9,13},{10,... | collective-permute-start | bytes 3145736 | tf_op jit(solution)/shard_map/ppermute | solution.py:51
  632.3 44.8 %collective-permute-start.83 = (bf16[4,128,2048]{2,1,0:T(8,128)(2,1)S(1)}, bf16[4,128,2048]{2,1,0:T(8,128)(2,1)S(1)}, u32[]{:S(2)}, u32[]{:S(2)}) collective-permute-start(bf16[4,128,2048]{2,1,0:T(8,128)(2,1)S(1)} %dynamic-slice_bitcast_fusion.3), channel_id=1, source_target_pairs={{0,4},{1,5},{2,6},{3,7},{4,0},{5,1},{6,2},{7,3},{8,12},{9,13},{10,... | collective-permute-start | bytes 6291464 | tf_op jit(solution)/shard_map/ppermute | solution.py:51
  636.5 19.3 %collective-permute-start.70 = (bf16[4,32,1024]{2,1,0:T(8,128)(2,1)S(1)}, bf16[4,32,1024]{2,1,0:T(8,128)(2,1)S(1)}, u32[]{:S(2)}, u32[]{:S(2)}) collective-permute-start(bf16[4,32,1024]{2,1,0:T(8,128)(2,1)S(1)} %get-tuple-element.68), channel_id=1, source_target_pairs={{0,2},{1,3},{2,0},{3,1},{4,6},{5,7},{6,4},{7,5},{8,10},{9,11},{10,... | collective-permute-start | bytes 786440 | tf_op jit(solution)/shard_map/ppermute | solution.py:48
  638.0 16.9 %collective-permute-start.78 = (bf16[4,32,1024]{2,1,0:T(8,128)(2,1)S(1)}, bf16[4,32,1024]{2,1,0:T(8,128)(2,1)S(1)}, u32[]{:S(2)}, u32[]{:S(2)}) collective-permute-start(bf16[4,32,1024]{2,1,0:T(8,128)(2,1)S(1)} %get-tuple-element.67), channel_id=1, source_target_pairs={{0,2},{1,3},{2,0},{3,1},{4,6},{5,7},{6,4},{7,5},{8,10},{9,11},{10,... | collective-permute-start | bytes 786440 | tf_op jit(solution)/shard_map/ppermute | solution.py:48
  664.1 65.7 %collective-permute-start.97 = (bf16[4,128,4096]{2,1,0:T(8,128)(2,1)}, bf16[4,128,4096]{2,1,0:T(8,128)(2,1)S(1)}, u32[]{:S(2)}, u32[]{:S(2)}) collective-permute-start(bf16[4,128,4096]{2,1,0:T(8,128)(2,1)} %dynamic-slice_bitcast_fusion.1), channel_id=1, source_target_pairs={{0,4},{1,5},{2,6},{3,7},{4,0},{5,1},{6,2},{7,3},{8,12},{9,13},{10,... | collective-permute-start | bytes 12582920 | tf_op jit(solution)/shard_map/ppermute | solution.py:51
  688.5 50.1 %collective-permute-start.104 = (bf16[4,512,1024]{2,1,0:T(8,128)(2,1)}, bf16[4,512,1024]{2,1,0:T(8,128)(2,1)}, u32[]{:S(2)}, u32[]{:S(2)}) collective-permute-start(bf16[4,512,1024]{2,1,0:T(8,128)(2,1)} %dynamic-slice_bitcast_fusion), channel_id=1, source_target_pairs={{0,4},{1,5},{2,6},{3,7},{4,0},{5,1},{6,2},{7,3},{8,12},{9,13},{10,... | collective-permute-start | bytes 12582920 | tf_op jit(solution)/shard_map/ppermute | solution.py:51
  700.4 28.2 %collective-permute-start.64 = (bf16[4,32,3072]{2,1,0:T(8,128)(2,1)S(1)}, bf16[4,32,3072]{2,1,0:T(8,128)(2,1)S(1)}, u32[]{:S(2)}, u32[]{:S(2)}) collective-permute-start(bf16[4,32,3072]{2,1,0:T(8,128)(2,1)S(1)} %get-tuple-element.55), channel_id=1, source_target_pairs={{0,1},{1,0},{2,3},{3,2},{4,5},{5,4},{6,7},{7,6},{8,9},{9,8},{10,11... | collective-permute-start | bytes 2359304 | tf_op jit(solution)/shard_map/ppermute | solution.py:48
  711.8 33.1 %collective-permute-start.63 = (bf16[4,32,3072]{2,1,0:T(8,128)(2,1)S(1)}, bf16[4,32,3072]{2,1,0:T(8,128)(2,1)}, u32[]{:S(2)}, u32[]{:S(2)}) collective-permute-start(bf16[4,32,3072]{2,1,0:T(8,128)(2,1)S(1)} %get-tuple-element.54), channel_id=1, source_target_pairs={{0,1},{1,0},{2,3},{3,2},{4,5},{5,4},{6,7},{7,6},{8,9},{9,8},{10,11... | collective-permute-start | bytes 2359304 | tf_op jit(solution)/shard_map/ppermute | solution.py:48
  713.6 70.7 %collective-permute-start.89 = (bf16[32,2048]{1,0:T(8,128)(2,1)}, bf16[32,2048]{1,0:T(8,128)(2,1)}, u32[]{:S(2)}, u32[]{:S(2)}) collective-permute-start(bf16[32,2048]{1,0:T(8,128)(2,1)} %get-tuple-element.74), channel_id=1, source_target_pairs={{0,24},{1,25},{2,26},{3,27},{4,28},{5,29},{6,30},{7,31},{8,0},{9,1... | collective-permute-start | bytes 393224 | tf_op jit(solution)/shard_map/ppermute | solution.py:43
  728.6 56.5 %collective-permute-start.88 = (bf16[32,2048]{1,0:T(8,128)(2,1)}, bf16[32,2048]{1,0:T(8,128)(2,1)}, u32[]{:S(2)}, u32[]{:S(2)}) collective-permute-start(bf16[32,2048]{1,0:T(8,128)(2,1)} %get-tuple-element.75), channel_id=1, source_target_pairs={{0,16},{1,17},{2,18},{3,19},{4,20},{5,21},{6,22},{7,23},{8,24},{9,... | collective-permute-start | bytes 393224 | tf_op jit(solution)/shard_map/ppermute | solution.py:43
  731.9 53.4 %collective-permute-start.87 = (bf16[32,2048]{1,0:T(8,128)(2,1)}, bf16[32,2048]{1,0:T(8,128)(2,1)}, u32[]{:S(2)}, u32[]{:S(2)}) collective-permute-start(bf16[32,2048]{1,0:T(8,128)(2,1)} %get-tuple-element.73), channel_id=1, source_target_pairs={{0,8},{1,9},{2,10},{3,11},{4,12},{5,13},{6,14},{7,15},{8,16},{9,17... | collective-permute-start | bytes 393224 | tf_op jit(solution)/shard_map/ppermute | solution.py:43
  738.6 20.6 %collective-permute-start.65 = (bf16[4,32,3072]{2,1,0:T(8,128)(2,1)S(1)}, bf16[4,32,3072]{2,1,0:T(8,128)(2,1)}, u32[]{:S(2)}, u32[]{:S(2)}) collective-permute-start(bf16[4,32,3072]{2,1,0:T(8,128)(2,1)S(1)} %fusion.37), channel_id=1, source_target_pairs={{0,2},{1,3},{2,0},{3,1},{4,6},{5,7},{6,4},{7,5},{8,10},{9,11},{10,... | collective-permute-start | bytes 2359304 | tf_op jit(solution)/shard_map/ppermute | solution.py:48
  744.9 36.7 %collective-permute-start.99 = (bf16[4,32,4096]{2,1,0:T(8,128)(2,1)S(1)}, bf16[4,32,4096]{2,1,0:T(8,128)(2,1)S(1)}, u32[]{:S(2)}, u32[]{:S(2)}) collective-permute-start(bf16[4,32,4096]{2,1,0:T(8,128)(2,1)S(1)} %get-tuple-element.53), channel_id=1, source_target_pairs={{0,2},{1,3},{2,0},{3,1},{4,6},{5,7},{6,4},{7,5},{8,10},{9,11},{10,... | collective-permute-start | bytes 3145736 | tf_op jit(solution)/shard_map/ppermute | solution.py:48
  759.2 53.3 %collective-permute-start.98 = (bf16[4,32,4096]{2,1,0:T(8,128)(2,1)S(1)}, bf16[4,32,4096]{2,1,0:T(8,128)(2,1)S(1)}, u32[]{:S(2)}, u32[]{:S(2)}) collective-permute-start(bf16[4,32,4096]{2,1,0:T(8,128)(2,1)S(1)} %get-tuple-element.52), channel_id=1, source_target_pairs={{0,2},{1,3},{2,0},{3,1},{4,6},{5,7},{6,4},{7,5},{8,10},{9,11},{10,... | collective-permute-start | bytes 3145736 | tf_op jit(solution)/shard_map/ppermute | solution.py:48
  784.3 26.2 %collective-permute-start.106 = (bf16[4,128,1024]{2,1,0:T(8,128)(2,1)S(1)}, bf16[4,128,1024]{2,1,0:T(8,128)(2,1)S(1)}, u32[]{:S(2)}, u32[]{:S(2)}) collective-permute-start(bf16[4,128,1024]{2,1,0:T(8,128)(2,1)S(1)} %get-tuple-element.51), channel_id=1, source_target_pairs={{0,1},{1,0},{2,3},{3,2},{4,5},{5,4},{6,7},{7,6},{8,9},{9,8},{10,11... | collective-permute-start | bytes 3145736 | tf_op jit(solution)/shard_map/ppermute | solution.py:48
  787.3 38.0 %collective-permute-start.100 = (bf16[4,32,4096]{2,1,0:T(8,128)(2,1)S(1)}, bf16[4,32,4096]{2,1,0:T(8,128)(2,1)S(1)}, u32[]{:S(2)}, u32[]{:S(2)}) collective-permute-start(bf16[4,32,4096]{2,1,0:T(8,128)(2,1)S(1)} %fusion.32), channel_id=1, source_target_pairs={{0,1},{1,0},{2,3},{3,2},{4,5},{5,4},{6,7},{7,6},{8,9},{9,8},{10,11... | collective-permute-start | bytes 3145736 | tf_op jit(solution)/shard_map/ppermute | solution.py:48
  795.1 41.4 %collective-permute-start.105 = (bf16[4,128,1024]{2,1,0:T(8,128)(2,1)S(1)}, bf16[4,128,1024]{2,1,0:T(8,128)(2,1)S(1)}, u32[]{:S(2)}, u32[]{:S(2)}) collective-permute-start(bf16[4,128,1024]{2,1,0:T(8,128)(2,1)S(1)} %get-tuple-element.50), channel_id=1, source_target_pairs={{0,1},{1,0},{2,3},{3,2},{4,5},{5,4},{6,7},{7,6},{8,9},{9,8},{10,11... | collective-permute-start | bytes 3145736 | tf_op jit(solution)/shard_map/ppermute | solution.py:48
  810.9 25.5 %collective-permute-start.107 = (bf16[4,128,1024]{2,1,0:T(8,128)(2,1)S(1)}, bf16[4,128,1024]{2,1,0:T(8,128)(2,1)S(1)}, u32[]{:S(2)}, u32[]{:S(2)}) collective-permute-start(bf16[4,128,1024]{2,1,0:T(8,128)(2,1)S(1)} %fusion.30), channel_id=1, source_target_pairs={{0,2},{1,3},{2,0},{3,1},{4,6},{5,7},{6,4},{7,5},{8,10},{9,11},{10,... | collective-permute-start | bytes 3145736 | tf_op jit(solution)/shard_map/ppermute | solution.py:48
  826.1 15.6 %collective-permute-start.102 = (bf16[32,4096]{1,0:T(8,128)(2,1)S(1)}, bf16[32,4096]{1,0:T(8,128)(2,1)S(1)}, u32[]{:S(2)}, u32[]{:S(2)}) collective-permute-start(bf16[32,4096]{1,0:T(8,128)(2,1)S(1)} %get-tuple-element.63), channel_id=1, source_target_pairs={{0,16},{1,17},{2,18},{3,19},{4,20},{5,21},{6,22},{7,23},{8,24},{9,... | collective-permute-start | bytes 786440 | tf_op jit(solution)/shard_map/ppermute | solution.py:43
  (142 other events, 2037.2 us)
